TPU v7x, 512 devices: a whole 4x8x8 slice. The times are simulated.
512 devices in a mesh: gx: 32 (over z, y_hi, core), gy: 16 (over y_lo, x).
Axes of the slice: x: 4, y: 8 (y_hi: 2, y_lo: 4; y = y_hi * 4 + y_lo), z: 8, core: 2. Of those that a mesh axis runs over, the one named last changes fastest.
Arguments:
- points: float32 [2, 96, 48, 32], P(None, 'gx', 'gy'), may hold values from 0 to 1
- diffusion: float32 [96, 48, 32], P('gx', 'gy'), may hold values from 0.05 to 0.5
- drift: float32 [2, 96, 48, 32], P(None, 'gx', 'gy'), may hold values from -4 to 4
- ionization: float32 [96, 48, 32], P('gx', 'gy'), may hold values from 0.2 to 2
- source: float32 [96, 48, 32], P('gx', 'gy'), may hold values from -32 to 32
- in_weight: bfloat16 [32, 16, 2, 256], P('gx', 'gy'), may hold values from -4 to 4
- in_bias: bfloat16 [32, 16, 256], P('gx', 'gy'), may hold values from -3 to 3
- mid_weight: bfloat16 [32, 16, 256, 256], P('gx', 'gy'), may hold values from -0.375 to 0.375
- mid_bias: bfloat16 [32, 16, 256], P('gx', 'gy'), may hold values from -3 to 3
- out_weight: bfloat16 [32, 16, 256], P('gx', 'gy'), may hold values from -0.375 to 0.375
Outputs:
- dir_in_weight: float32 [32, 16, 2, 256], P('gx', 'gy')
- dir_in_bias: float32 [32, 16, 256], P('gx', 'gy')
- dir_mid_weight: float32 [32, 16, 256, 256], P('gx', 'gy')
- dir_mid_bias: float32 [32, 16, 256], P('gx', 'gy')
- dir_out_weight: float32 [32, 16, 256], P('gx', 'gy')
- loss: float32 [], replicated
All inputs are finite; a program needn't handle non-finite values.
Results may differ from a plain program's by a relative error of at most 0.0012.
Values may be sent and summed in bfloat16 or wider, within the bound.
No kernel may reach another device: no remote copies, remote signals or barrier semaphores. Data moves between devices by JAX's collectives and lax.ppermute only.
A program may use at most 64 MiB of HBM per device.

v0:
```python
import jax
import jax.numpy as jnp
from jax import lax
from jax.sharding import PartitionSpec as P

DELTA = 0.25
EPS = 1e-06


def extended(block, sides, width):
    for axis, dim in sides:
        count = lax.axis_size(axis)
        forward = [(i, i + 1) for i in range(count - 1)]
        forward.append((count - 1, 0))
        backward = [(target, source) for source, target in forward]
        low = lax.ppermute(
            lax.slice_in_dim(block, block.shape[dim] - width, None, axis=dim), axis, forward
        )
        high = lax.ppermute(lax.slice_in_dim(block, 0, width, axis=dim), axis, backward)
        block = jnp.concatenate([low, block, high], axis=dim)
    return block


def region_frame(index):
    low = jnp.where(index == 0, 0.0, jnp.where(index == 1, DELTA, 1.0 - DELTA)).astype(jnp.float32)
    extent = jnp.where(index == 1, 1.0 - 2.0 * DELTA, DELTA).astype(jnp.float32)
    return (low, extent)


def smooth_rise(coord):
    ramp = jnp.clip((coord + DELTA) / (2.0 * DELTA), 0.0, 1.0)
    value = ramp * ramp * ramp * (10.0 - 15.0 * ramp + 6.0 * ramp * ramp)
    slope = 30.0 * ramp * ramp * (1.0 - ramp) * (1.0 - ramp) / (2.0 * DELTA)
    bend = 60.0 * ramp * (1.0 - ramp) * (1.0 - 2.0 * ramp) / (4.0 * DELTA * DELTA)
    return (value, slope, bend)


def bump(coord):
    rise_a = smooth_rise(coord)
    rise_b = smooth_rise(coord - 1.0)
    return (rise_a[0] - rise_b[0], rise_a[1] - rise_b[1], rise_a[2] - rise_b[2])


def coefficients(coord_x, coord_y, present, diff, vel_x, vel_y, rate):
    bump_x = bump(coord_x)
    bump_y = bump(coord_y)
    window = bump_x[0] * bump_y[0] * present
    window_x = bump_x[1] * bump_y[0] * present
    window_y = bump_x[0] * bump_y[1] * present
    window_l = (bump_x[2] * bump_y[0] + bump_x[0] * bump_y[2]) * present
    c_val = -diff * window_l + vel_x * window_x + vel_y * window_y - rate * window
    c_dx = -2.0 * diff * window_x + vel_x * window
    c_dy = -2.0 * diff * window_y + vel_y * window
    c_lap = -diff * window
    return (c_val, c_dx, c_dy, c_lap)


def net_state(params, coord_x, coord_y):
    w_in, b_in, w_mid, b_mid, w_out = params
    w_first = w_in[0].astype(jnp.float32)
    w_second = w_in[1].astype(jnp.float32)
    across = (2.0 * coord_x - 1.0)[:, None]
    along = (2.0 * coord_y - 1.0)[:, None]
    hid_one = jnp.tanh(across * w_first + along * w_second + b_in.astype(jnp.float32))
    damp_one = 1.0 - hid_one * hid_one
    power = w_first * w_first + w_second * w_second
    streams = jnp.concatenate(
        [
            hid_one,
            2.0 * damp_one * w_first,
            2.0 * damp_one * w_second,
            -8.0 * hid_one * damp_one * power,
        ],
        axis=0,
    ).astype(jnp.bfloat16)
    mixed = jnp.dot(streams, w_mid, preferred_element_type=jnp.float32)
    count = coord_x.shape[0]
    grad_x = mixed[count : 2 * count]
    grad_y = mixed[2 * count : 3 * count]
    curve = mixed[3 * count :]
    hid_two = jnp.tanh(mixed[:count] + b_mid.astype(jnp.float32))
    return dict(
        across=across,
        along=along,
        hid_one=hid_one,
        streams=streams,
        grad_x=grad_x,
        grad_y=grad_y,
        curve=curve,
        hid_two=hid_two,
    )


def net_outputs(state):
    hid_two = state["hid_two"]
    damp_two = 1.0 - hid_two * hid_two
    grad_x = state["grad_x"]
    grad_y = state["grad_y"]
    square = grad_x * grad_x + grad_y * grad_y
    return (
        hid_two,
        damp_two * grad_x,
        damp_two * grad_y,
        -2.0 * hid_two * damp_two * square + damp_two * state["curve"],
    )


def net_fields(params, state):
    head = params[4].astype(jnp.float32)
    return tuple(
        (jnp.dot(out_k, head, precision=lax.Precision.HIGHEST) for out_k in net_outputs(state))
    )


def combine(factors, fields):
    return (
        factors[0] * fields[0]
        + factors[1] * fields[1]
        + factors[2] * fields[2]
        + factors[3] * fields[3]
    )


def net_backward(params, state, cots):
    w_mid = params[2]
    head = params[4].astype(jnp.float32)
    w_first = params[0][0].astype(jnp.float32)
    w_second = params[0][1].astype(jnp.float32)
    power = w_first * w_first + w_second * w_second
    outputs = net_outputs(state)
    d_out = jnp.dot(cots[0], outputs[0], precision=lax.Precision.HIGHEST)
    for index in range(1, 4):
        d_out = d_out + jnp.dot(cots[index], outputs[index], precision=lax.Precision.HIGHEST)
    d_o = [cot_k[:, None] * head for cot_k in cots]
    hid_two = state["hid_two"]
    damp_two = 1.0 - hid_two * hid_two
    grad_x = state["grad_x"]
    grad_y = state["grad_y"]
    square = grad_x * grad_x + grad_y * grad_y
    d_damp = d_o[1] * grad_x + d_o[2] * grad_y + (-2.0 * hid_two * square + state["curve"]) * d_o[3]
    d_hid = d_o[0] - 2.0 * damp_two * square * d_o[3] - 2.0 * hid_two * d_damp
    d_base = d_hid * damp_two
    d_gx = d_o[1] * damp_two - 4.0 * hid_two * damp_two * grad_x * d_o[3]
    d_gy = d_o[2] * damp_two - 4.0 * hid_two * damp_two * grad_y * d_o[3]
    d_curve = damp_two * d_o[3]
    d_bmid = jnp.sum(d_base, axis=0)
    d_mixed = jnp.concatenate([d_base, d_gx, d_gy, d_curve], axis=0).astype(jnp.bfloat16)
    d_wmid = lax.dot_general(
        state["streams"], d_mixed, (((0,), (0,)), ((), ())), preferred_element_type=jnp.float32
    )
    d_streams = lax.dot_general(
        d_mixed, w_mid, (((1,), (1,)), ((), ())), preferred_element_type=jnp.float32
    )
    count = hid_two.shape[0]
    ds_zero = d_streams[:count]
    ds_one = d_streams[count : 2 * count]
    ds_two = d_streams[2 * count : 3 * count]
    ds_three = d_streams[3 * count :]
    hid_one = state["hid_one"]
    damp_one = 1.0 - hid_one * hid_one
    d_damp1 = 2.0 * w_first * ds_one + 2.0 * w_second * ds_two - 8.0 * hid_one * power * ds_three
    d_hid1 = ds_zero - 8.0 * damp_one * power * ds_three - 2.0 * hid_one * d_damp1
    d_pre = d_hid1 * damp_one
    d_first = jnp.sum(
        2.0 * damp_one * ds_one
        - 16.0 * hid_one * damp_one * w_first * ds_three
        + state["across"] * d_pre,
        axis=0,
    )
    d_second = jnp.sum(
        2.0 * damp_one * ds_two
        - 16.0 * hid_one * damp_one * w_second * ds_three
        + state["along"] * d_pre,
        axis=0,
    )
    d_bin = jnp.sum(d_pre, axis=0)
    return (jnp.stack([d_first, d_second], axis=0), d_bin, d_wmid, d_bmid, d_out)


def region_slice(shift):
    if shift == 0:
        return (0, 3)
    return (1 + shift, 2 + shift)


def unpack_net(block):
    hidden = block.shape[-1]
    return (block[0:2], block[2], block[3 : 3 + hidden], block[3 + hidden], block[4 + hidden])


def pack_terms(terms):
    return jnp.concatenate(
        [terms[0], terms[1][None], terms[2], terms[3][None], terms[4][None]], axis=0
    )


def local(
    points,
    diffusion,
    drift,
    ionization,
    source,
    in_weight,
    in_bias,
    mid_weight,
    mid_bias,
    out_weight,
):
    span = points.shape[-1]
    hidden = mid_weight.shape[-1]
    column = lax.axis_index("gx")
    columns = lax.axis_size("gx")
    nets = columns * lax.axis_size("gy")
    low, width = region_frame(jnp.arange(3, dtype=jnp.int32))
    pos_x = low[:, None, None] + width[:, None, None] * points[0]
    pos_y = low[None, :, None] + width[None, :, None] * points[1]
    area = width[:, None, None] * width[None, :, None] / span * jnp.ones_like(pos_x)
    packed = jnp.concatenate(
        [in_weight, in_bias[:, :, None], mid_weight, mid_bias[:, :, None], out_weight[:, :, None]],
        axis=2,
    )
    neighbours = extended(packed, (("gx", 0), ("gy", 1)), 1)
    totals = jnp.zeros_like(pos_x)
    saved = {}
    for shift_x in (-1, 0, 1):
        for shift_y in (-1, 0, 1):
            lo_x, hi_x = region_slice(shift_x)
            lo_y, hi_y = region_slice(shift_y)
            params = unpack_net(neighbours[shift_x + 1, shift_y + 1])
            coord_x = (pos_x[lo_x:hi_x, lo_y:hi_y] - float(shift_x)).reshape(-1)
            coord_y = (pos_y[lo_x:hi_x, lo_y:hi_y] - float(shift_y)).reshape(-1)
            neighbour = column + shift_x
            present = ((neighbour >= 0) & (neighbour < columns)).astype(jnp.float32)
            factors = coefficients(
                coord_x,
                coord_y,
                present,
                diffusion[lo_x:hi_x, lo_y:hi_y].reshape(-1),
                drift[0, lo_x:hi_x, lo_y:hi_y].reshape(-1),
                drift[1, lo_x:hi_x, lo_y:hi_y].reshape(-1),
                ionization[lo_x:hi_x, lo_y:hi_y].reshape(-1),
            )
            state = net_state(params, coord_x, coord_y)
            contrib = combine(factors, net_fields(params, state))
            totals = totals.at[lo_x:hi_x, lo_y:hi_y].add(
                contrib.reshape(hi_x - lo_x, hi_y - lo_y, span)
            )
            saved[shift_x, shift_y] = (params, state, factors)
    residual = totals - source
    loss_local = jnp.sum(area * residual * residual)
    adjoint = 2.0 * area * residual
    loss = lax.psum(loss_local, ("gx", "gy"))
    rows_x = []
    for shift_x in (-1, 0, 1):
        row_terms = []
        for shift_y in (-1, 0, 1):
            lo_x, hi_x = region_slice(shift_x)
            lo_y, hi_y = region_slice(shift_y)
            params, state, factors = saved[shift_x, shift_y]
            weight_here = adjoint[lo_x:hi_x, lo_y:hi_y].reshape(-1)
            cots = tuple((weight_here * factor for factor in factors))
            row_terms.append(pack_terms(net_backward(params, state, cots)))
        rows_x.append(jnp.stack(row_terms, axis=0))
    grads = jnp.stack(rows_x, axis=0)
    outward = jnp.stack([grads[0], grads[2]], axis=0)
    inward = extended(outward, (("gx", 0),), 1)
    middle = grads[1] + inward[0] + inward[3]
    upward = jnp.stack([middle[0], middle[2]], axis=0)
    arrived = extended(upward, (("gy", 0),), 1)
    own_grads = unpack_net(middle[1] + arrived[0] + arrived[3])
    square_local = jnp.sum(own_grads[0] * own_grads[0])
    for index in range(1, 5):
        square_local = square_local + jnp.sum(own_grads[index] * own_grads[index])
    square = lax.psum(square_local, ("gx", "gy"))
    rms = jnp.sqrt(square / (nets * (hidden * hidden + 5 * hidden)) + EPS)
    results = tuple(((grad / rms)[None, None] for grad in own_grads))
    return (results[0], results[1], results[2], results[3], results[4], loss)


def solution(mesh):
    return jax.shard_map(
        local,
        mesh=mesh,
        in_specs=(
            P(None, "gx", "gy", None),
            P("gx", "gy", None),
            P(None, "gx", "gy", None),
            P("gx", "gy", None),
            P("gx", "gy", None),
            P("gx", "gy", None, None),
            P("gx", "gy", None),
            P("gx", "gy", None, None),
            P("gx", "gy", None),
            P("gx", "gy", None),
        ),
        out_specs=(
            P("gx", "gy", None, None),
            P("gx", "gy", None),
            P("gx", "gy", None, None),
            P("gx", "gy", None),
            P("gx", "gy", None),
            P(),
        ),
        check_vma=False,
    )
```

profile of v0, /device:TPU:1, one launch (start us, length us, event | category | flops | bytes accessed | tf_op | source)
XLA Modules:
  0.0 364.4 jit_solution(7670948863165979024)
XLA Ops:
  0.6 2.6 concatenate.127
  3.2 8.8 %collective-permute-start.1 = (bf16[1,1,261,256]{3,2,1,0:T(8,128)(2,1)S(1)}, bf16[1,1,261,256]{3,2,1,0:T(8,128)(2,1)S(1)}, u32[]{:S(2)}, u32[]{:S(2)}) collective-permute-start(bf16[1,1,261,256]{3,2,1,0:T(8,128)(2,1)S(1)} %concatenate.127), channel_id=1, source_target_pairs={{16,0},{32,16},{48,32},{64,48},{80,64},{96,80},{112,96},{128,112},... | collective-permute-start | bytes 400904 | tf_op jit(solution)/shard_map/ppermute | solution.py:19
  12.0 2.0 collective-permute-start
  45.5 7.0 %collective-permute-start.3 = (bf16[3,1,261,256]{3,2,1,0:T(8,128)(2,1)S(1)}, bf16[3,1,261,256]{3,2,1,0:T(8,128)(2,1)}, u32[]{:S(2)}, u32[]{:S(2)}) collective-permute-start(bf16[3,1,261,256]{3,2,1,0:T(8,128)(2,1)S(1)} %pad_maximum_fusion.2), channel_id=1, source_target_pairs={{1,0},{2,1},{3,2},{4,3},{5,4},{6,5},{7,6},{8,7},{9,8},{10,9},{11,1... | collective-permute-start | bytes 1202696 | tf_op jit(solution)/shard_map/ppermute | solution.py:19
  52.5 1.9 collective-permute-start.2
  61.5 2.0 slice_reduce_fusion.14
  83.1 2.7 fusion.63
  143.3 2.1 fusion.823
  146.9 2.1 fusion.833
  150.4 2.0 fusion.829
  153.8 2.0 fusion.827
  159.2 1.9 fusion.837
  175.5 2.1 fusion.835
  192.6 1.7 copy.25
  194.3 2.2 collective-permute-start.4
  196.5 8.2 %collective-permute-start.5 = (f32[1,3,261,256]{3,0,2,1:T(1,128)S(1)}, f32[1,3,261,256]{3,0,2,1:T(1,128)}, u32[]{:S(2)}, u32[]{:S(2)}) collective-permute-start(f32[1,3,261,256]{3,0,2,1:T(1,128)S(1)} %copy.26), channel_id=1, source_target_pairs={{16,0},{32,16},{48,32},{64,48},{80,64},{96,80},{112,96},{128,112},... | collective-permute-start | bytes 2405384 | tf_op jit(solution)/shard_map/ppermute | solution.py:19
  212.7 1.8 concatenate.140
  217.2 12.9 %collective-permute-done.5 = f32[1,3,261,256]{3,0,2,1:T(1,128)} collective-permute-done((f32[1,3,261,256]{3,0,2,1:T(1,128)S(1)}, f32[1,3,261,256]{3,0,2,1:T(1,128)}, u32[]{:S(2)}, u32[]{:S(2)}) %collective-permute-start.5) | collective-permute-done | bytes 801824 | tf_op jit(solution)/shard_map/ppermute | solution.py:19
  230.1 1.5 fusion.64
  231.7 8.0 %collective-permute-start.6 = (f32[1,261,256]{2,1,0:T(8,128)S(1)}, f32[1,261,256]{2,1,0:T(8,128)S(1)}, u32[]{:S(2)}, u32[]{:S(2)}) collective-permute-start(f32[1,261,256]{2,1,0:T(8,128)S(1)} %get-tuple-element.274), channel_id=1, source_target_pairs={{0,1},{1,2},{2,3},{3,4},{4,5},{5,6},{6,7},{7,8},{8,9},{9,10},{10,1... | collective-permute-start | bytes 801800 | tf_op jit(solution)/shard_map/ppermute | solution.py:16
  239.7 1.9 collective-permute-start.7
  241.7 3.5 collective-permute-done.6
  245.2 4.1 %collective-permute-done.7 = f32[1,261,256]{2,1,0:T(8,128)S(1)} collective-permute-done((f32[1,261,256]{2,1,0:T(8,128)S(1)}, f32[1,261,256]{2,1,0:T(8,128)S(1)}, u32[]{:S(2)}, u32[]{:S(2)}) %collective-permute-start.7) | collective-permute-done | bytes 267296 | tf_op jit(solution)/shard_map/ppermute | solution.py:19
  254.5 107.3 %all-reduce.1 = (f32[]{:T(128)}, f32[]{:T(128)}) all-reduce(f32[]{:T(128)S(6)} %add.3003, f32[]{:T(128)} %get-tuple-element.357), channel_id=1, replica_groups=mesh['gx'=32,'gy'=16] {'gx','gy'}, use_global_device_ids=true, to_apply=%region_42.43 | all-reduce | flops 2 | bytes 16 | tf_op jit(solution)/shard_map/psum | solution.py:274
  (978 shorter events, 162.8 us)
Async XLA Ops:
  0.6 27.8 %copy-start.23 = (bf16[1,1,256,256]{3,2,1,0:T(8,128)(2,1)S(1)}, bf16[1,1,256,256]{3,2,1,0:T(8,128)(2,1)}, u32[]{:S(2)}) copy-start(bf16[1,1,256,256]{3,2,1,0:T(8,128)(2,1)} %param.37) | copy-start | bytes 393220
  3.2 42.2 %collective-permute-start.1 = (bf16[1,1,261,256]{3,2,1,0:T(8,128)(2,1)S(1)}, bf16[1,1,261,256]{3,2,1,0:T(8,128)(2,1)S(1)}, u32[]{:S(2)}, u32[]{:S(2)}) collective-permute-start(bf16[1,1,261,256]{3,2,1,0:T(8,128)(2,1)S(1)} %concatenate.127), channel_id=1, source_target_pairs={{16,0},{32,16},{48,32},{64,48},{80,64},{96,80},{112,96},{128,112},... | collective-permute-start | bytes 400904 | tf_op jit(solution)/shard_map/ppermute | solution.py:19
  12.0 33.5 %collective-permute-start = (bf16[1,1,261,256]{3,2,1,0:T(8,128)(2,1)S(1)}, bf16[1,1,261,256]{3,2,1,0:T(8,128)(2,1)S(1)}, u32[]{:S(2)}, u32[]{:S(2)}) collective-permute-start(bf16[1,1,261,256]{3,2,1,0:T(8,128)(2,1)S(1)} %concatenate.127), channel_id=1, source_target_pairs={{0,16},{16,32},{32,48},{48,64},{64,80},{80,96},{96,112},{112,128},... | collective-permute-start | bytes 400904 | tf_op jit(solution)/shard_map/ppermute | solution.py:16
  39.0 21.5 %copy-start.249 = (f32[96]{0:T(128)}, f32[96]{0:T(128)S(1)}, u32[]{:S(2)}) copy-start(f32[96]{0:T(128)S(1)} %get-tuple-element.263) | copy-start | bytes 1156
  39.1 21.0 %copy-start.305 = (f32[96]{0:T(128)}, f32[96]{0:T(128)S(1)}, u32[]{:S(2)}) copy-start(f32[96]{0:T(128)S(1)} %get-tuple-element.480) | copy-start | bytes 1156
  39.1 21.1 %copy-start.303 = (f32[96]{0:T(128)}, f32[96]{0:T(128)S(1)}, u32[]{:S(2)}) copy-start(f32[96]{0:T(128)S(1)} %get-tuple-element.479) | copy-start | bytes 1156
  39.1 21.3 %copy-start.254 = (f32[96]{0:T(128)}, f32[96]{0:T(128)S(1)}, u32[]{:S(2)}) copy-start(f32[96]{0:T(128)S(1)} %get-tuple-element.510) | copy-start | bytes 1156
  42.3 21.7 %copy-start.234 = (f32[96]{0:T(128)}, f32[96]{0:T(128)S(1)}, u32[]{:S(2)}) copy-start(f32[96]{0:T(128)S(1)} %sub.2540) | copy-start | bytes 1156
  43.7 20.3 %copy-start.236 = (f32[96]{0:T(128)}, f32[96]{0:T(128)S(1)}, u32[]{:S(2)}) copy-start(f32[96]{0:T(128)S(1)} %sub.2537) | copy-start | bytes 1156
  45.5 16.0 %collective-permute-start.3 = (bf16[3,1,261,256]{3,2,1,0:T(8,128)(2,1)S(1)}, bf16[3,1,261,256]{3,2,1,0:T(8,128)(2,1)}, u32[]{:S(2)}, u32[]{:S(2)}) collective-permute-start(bf16[3,1,261,256]{3,2,1,0:T(8,128)(2,1)S(1)} %pad_maximum_fusion.2), channel_id=1, source_target_pairs={{1,0},{2,1},{3,2},{4,3},{5,4},{6,5},{7,6},{8,7},{9,8},{10,9},{11,1... | collective-permute-start | bytes 1202696 | tf_op jit(solution)/shard_map/ppermute | solution.py:19
  52.5 20.1 %collective-permute-start.2 = (bf16[3,1,261,256]{3,2,1,0:T(8,128)(2,1)S(1)}, bf16[3,1,261,256]{3,2,1,0:T(8,128)(2,1)}, u32[]{:S(2)}, u32[]{:S(2)}) collective-permute-start(bf16[3,1,261,256]{3,2,1,0:T(8,128)(2,1)S(1)} %pad_maximum_fusion.2), channel_id=1, source_target_pairs={{0,1},{1,2},{2,3},{3,4},{4,5},{5,6},{6,7},{7,8},{8,9},{9,10},{10,1... | collective-permute-start | bytes 1202696 | tf_op jit(solution)/shard_map/ppermute | solution.py:16
  74.0 20.1 %copy-start.97 = (f32[1,1,1,256]{3,2,1,0:T(1,128)}, f32[1,1,1,256]{3,2,1,0:T(1,128)S(1)}, u32[]{:S(2)}) copy-start(f32[1,1,1,256]{3,2,1,0:T(1,128)S(1)} %get-tuple-element.278) | copy-start | bytes 3076
  74.1 20.0 %copy-start.99 = (f32[1,1,1,256]{3,2,1,0:T(1,128)}, f32[1,1,1,256]{3,2,1,0:T(1,128)S(1)}, u32[]{:S(2)}) copy-start(f32[1,1,1,256]{3,2,1,0:T(1,128)S(1)} %get-tuple-element.279) | copy-start | bytes 3076
  74.1 22.0 %copy-start.76 = (f32[1,1,1,256]{3,2,1,0:T(1,128)}, f32[1,1,1,256]{3,2,1,0:T(1,128)S(1)}, u32[]{:S(2)}) copy-start(f32[1,1,1,256]{3,2,1,0:T(1,128)S(1)} %get-tuple-element.276) | copy-start | bytes 3076
  116.7 37.1 %copy-start.246 = (f32[32]{0:T(128)S(1)}, f32[32]{0:T(128)}, u32[]{:S(2)}) copy-start(f32[32]{0:T(128)} %get-tuple-element.361) | copy-start | bytes 388
  118.1 32.3 %copy-start.1 = (f32[128,256]{1,0:T(8,128)S(1)}, f32[128,256]{1,0:T(8,128)}, u32[]{:S(2)}) copy-start(f32[128,256]{1,0:T(8,128)} %copy-done) | copy-start | bytes 393220
  118.1 34.3 %copy-start.5 = (f32[128,256]{1,0:T(8,128)S(1)}, f32[128,256]{1,0:T(8,128)}, u32[]{:S(2)}) copy-start(f32[128,256]{1,0:T(8,128)} %copy-done.4) | copy-start | bytes 393220
  118.1 34.3 %copy-start.247 = (f32[32]{0:T(128)S(1)}, f32[32]{0:T(128)}, u32[]{:S(2)}) copy-start(f32[32]{0:T(128)} %get-tuple-element.382) | copy-start | bytes 388
  118.1 35.7 %copy-start.299 = (f32[32]{0:T(128)S(1)}, f32[32]{0:T(128)}, u32[]{:S(2)}) copy-start(f32[32]{0:T(128)} %get-tuple-element.376) | copy-start | bytes 388
  118.1 35.7 %copy-start.300 = (f32[32]{0:T(128)S(1)}, f32[32]{0:T(128)}, u32[]{:S(2)}) copy-start(f32[32]{0:T(128)} %get-tuple-element.377) | copy-start | bytes 388
  194.3 22.8 %collective-permute-start.4 = (f32[1,3,261,256]{3,0,2,1:T(1,128)}, f32[1,3,261,256]{3,0,2,1:T(1,128)}, u32[]{:S(2)}, u32[]{:S(2)}) collective-permute-start(f32[1,3,261,256]{3,0,2,1:T(1,128)} %copy.25), channel_id=1, source_target_pairs={{0,16},{16,32},{32,48},{48,64},{64,80},{80,96},{96,112},{112,128},... | collective-permute-start | bytes 2405384 | tf_op jit(solution)/shard_map/ppermute | solution.py:16
  196.5 33.6 %collective-permute-start.5 = (f32[1,3,261,256]{3,0,2,1:T(1,128)S(1)}, f32[1,3,261,256]{3,0,2,1:T(1,128)}, u32[]{:S(2)}, u32[]{:S(2)}) collective-permute-start(f32[1,3,261,256]{3,0,2,1:T(1,128)S(1)} %copy.26), channel_id=1, source_target_pairs={{16,0},{32,16},{48,32},{64,48},{80,64},{96,80},{112,96},{128,112},... | collective-permute-start | bytes 2405384 | tf_op jit(solution)/shard_map/ppermute | solution.py:19
  231.7 13.5 %collective-permute-start.6 = (f32[1,261,256]{2,1,0:T(8,128)S(1)}, f32[1,261,256]{2,1,0:T(8,128)S(1)}, u32[]{:S(2)}, u32[]{:S(2)}) collective-permute-start(f32[1,261,256]{2,1,0:T(8,128)S(1)} %get-tuple-element.274), channel_id=1, source_target_pairs={{0,1},{1,2},{2,3},{3,4},{4,5},{5,6},{6,7},{7,8},{8,9},{9,10},{10,1... | collective-permute-start | bytes 801800 | tf_op jit(solution)/shard_map/ppermute | solution.py:16
  239.7 9.6 %collective-permute-start.7 = (f32[1,261,256]{2,1,0:T(8,128)S(1)}, f32[1,261,256]{2,1,0:T(8,128)S(1)}, u32[]{:S(2)}, u32[]{:S(2)}) collective-permute-start(f32[1,261,256]{2,1,0:T(8,128)S(1)} %get-tuple-element.275), channel_id=1, source_target_pairs={{1,0},{2,1},{3,2},{4,3},{5,4},{6,5},{7,6},{8,7},{9,8},{10,9},{11,1... | collective-permute-start | bytes 801800 | tf_op jit(solution)/shard_map/ppermute | solution.py:19
  (315 other events, 1312.8 us)
where the time goes:
time: 368 us; the launch traced here: 364 us
  blocking collectives  107 us (29%)
  matrix products  80.2 us (22%)
  other arithmetic  69.3 us (19%)
  starting transfers between devices  40 us (11%)
  local copies, waits for them, and re-layouts  37.8 us (10%)
  waiting for transfers between devices  20.6 us (6%)
  between operations  9.29 us (3%)
    psum x1, blocking collectives, local(): square = lax.psum(square_local, ('gx', 'gy'))  107 us
    dot_general x27, matrix products, net_backward(): jnp.dot(cots[index], outputs[index], precision=lax.Precision.HIGHEST)  26.7 us
    dot_general x36, matrix products, net_fields(): jnp.dot(out_k, head, precision=lax.Precision.HIGHEST)  25.9 us
    ppermute x4, starting transfers between devices, extended(): lax.ppermute(lax.slice_in_dim(block, 0, width, axis=dim), axis, backward)  25.9 us
    ppermute x4, waiting for transfers between devices, extended(): lax.ppermute(lax.slice_in_dim(block, 0, width, axis=dim), axis, backward)  17 us
    ppermute x4, starting transfers between devices, extended(): lax.ppermute(lax.slice_in_dim(block, block.shape[dim] - width, None, axis...  14.1 us
    reduce_sum x9, other arithmetic, net_backward(): d_bmid = jnp.sum(d_base, axis=0)  13.9 us
    dot_general x9, matrix products, net_backward(): d_out = jnp.dot(cots[0], outputs[0], precision=lax.Precision.HIGHEST)  9.57 us
  transfers between devices with their start and end apart: 8, of which 3 were waited for; matrix products, arithmetic and copies ran while one was open for 16% of the time, Pallas kernels for 0%

commit v1 on v0

v1 whole, which is shorter than its diff:
```python
import jax
import jax.numpy as jnp
from jax import lax
from jax.experimental import pallas as pl
from jax.experimental.pallas import tpu as pltpu
from jax.sharding import Mesh, PartitionSpec as P

DELTA = 0.25
EPS = 1e-06
H = 256
LANES = 128
SPAN = 32
ROWS = 288
F32 = jnp.float32
BF16 = jnp.bfloat16

CHUNKS = (
    ((0, 0), (0, 1), (1, 0), (1, 1)),
    ((0, 3), (0, 4), (1, 3), (1, 4)),
    ((3, 0), (3, 1), (4, 0), (4, 1)),
    ((3, 3), (3, 4), (4, 3), (4, 4)),
    ((0, 2), (1, 2), (3, 2), (4, 2)),
    ((2, 0), (2, 1), (2, 3), (2, 4)),
    ((2, 2),),
)
PLACE = {
    (0, 0): 0,
    (0, 1): 32,
    (0, 2): 64,
    (1, 0): 96,
    (2, 0): 128,
    (2, 1): 160,
    (2, 2): 192,
    (1, 2): 224,
    (1, 1): 256,
}
LOW = (0.0, DELTA, 1.0 - DELTA)
WIDTH = (DELTA, 1.0 - 2.0 * DELTA, DELTA)


def smooth_rise(coord):
    ramp = jnp.clip((coord + DELTA) / (2.0 * DELTA), 0.0, 1.0)
    value = ramp * ramp * ramp * (10.0 - 15.0 * ramp + 6.0 * ramp * ramp)
    slope = 30.0 * ramp * ramp * (1.0 - ramp) * (1.0 - ramp) / (2.0 * DELTA)
    bend = 60.0 * ramp * (1.0 - ramp) * (1.0 - 2.0 * ramp) / (4.0 * DELTA * DELTA)
    return (value, slope, bend)


def bump(coord):
    rise_a = smooth_rise(coord)
    rise_b = smooth_rise(coord - 1.0)
    return (rise_a[0] - rise_b[0], rise_a[1] - rise_b[1], rise_a[2] - rise_b[2])


def pack_kernel(
    pts, dif, dri, ion, src, w_in, b_in, w_mid, b_mid, w_out, pay_ref, tab_ref
):
    zeros = jnp.zeros((1, SPAN), F32)
    ones = jnp.ones((1, SPAN), F32)
    pieces = {}
    for a in range(3):
        for b in range(3):
            rows = [
                LOW[a] + WIDTH[a] * pts[0, a, b : b + 1, :],
                LOW[b] + WIDTH[b] * pts[1, a, b : b + 1, :],
                dif[a, b : b + 1, :],
                dri[0, a, b : b + 1, :],
                dri[1, a, b : b + 1, :],
                ion[a, b : b + 1, :],
                src[a, b : b + 1, :],
                ones,
            ]
            pieces[PLACE[a, b]] = jnp.concatenate(rows, axis=0)
    blank = jnp.concatenate([zeros] * 8, axis=0)
    order = [pieces.get(32 * k, blank) for k in range(12)]
    tabs = [jnp.concatenate(order[4 * k : 4 * k + 4], axis=1) for k in range(3)]
    for k in range(3):
        tab_ref[:, 128 * k : 128 * k + 128] = tabs[k]
    edge = jnp.concatenate(tabs[:2], axis=1)
    high = edge.astype(BF16).astype(F32)
    rest = edge - high
    mid = rest.astype(BF16).astype(F32)
    low = rest - mid
    small = jnp.concatenate(
        [
            w_in[0, 0].astype(F32),
            b_in[0].astype(F32),
            b_mid[0].astype(F32),
            w_out[0].astype(F32),
            jnp.ones((1, H), F32),
            jnp.zeros((2, H), F32),
        ],
        axis=0,
    )
    pay_ref[H:ROWS, :] = jnp.concatenate([high, mid, low, small], axis=0).astype(BF16)
    pay_ref[0:H, :] = jnp.transpose(w_mid[0, 0].astype(F32)).astype(BF16)


def small_rows(ref, index):
    return ref[index, H:ROWS, :].astype(F32)


def columns_of(small):
    w_first, w_second = small[24:25], small[25:26]
    power = w_first * w_first + w_second * w_second
    rows = jnp.concatenate(
        [
            w_first,
            w_second,
            small[26:27],
            2.0 * w_first,
            2.0 * w_second,
            -8.0 * power,
            small[27:28],
            small[28:29],
        ],
        axis=0,
    )
    return jnp.transpose(rows)


def forward(cols, weights, xi, eta):
    h1 = jnp.tanh(xi * cols[:, 0:1] + eta * cols[:, 1:2] + cols[:, 2:3])
    d1 = 1.0 - h1 * h1
    streams = jnp.concatenate(
        [
            h1.astype(BF16),
            (d1 * cols[:, 3:4]).astype(BF16),
            (d1 * cols[:, 4:5]).astype(BF16),
            (h1 * d1 * cols[:, 5:6]).astype(BF16),
        ],
        axis=1,
    )
    mixed = jnp.dot(weights, streams, preferred_element_type=F32)
    h2 = jnp.tanh(mixed[:, 0:LANES] + cols[:, 6:7])
    gx = mixed[:, LANES : 2 * LANES]
    gy = mixed[:, 2 * LANES : 3 * LANES]
    curve = mixed[:, 3 * LANES :]
    return h1, streams, h2, gx, gy, curve


def output_mix(c, h2, gx, gy, curve):
    d2 = 1.0 - h2 * h2
    square = gx * gx + gy * gy
    return c[0] * h2 + d2 * (
        c[1] * gx + c[2] * gy + c[3] * (curve - 2.0 * h2 * square)
    )


def select(step, values):
    out = jnp.int32(values[0])
    for k in range(1, len(values)):
        out = jnp.where(step == k, jnp.int32(values[k]), out)
    return out


def net_kernel(
    mid_ref,
    lo_ref,
    hi_ref,
    tab_ref,
    w_ref,
    gw_ref,
    gs_ref,
    stat_ref,
    chunk_ref,
    coef_ref,
    total_ref,
    col_ref,
    h1_ref,
    s_ref,
    h2_ref,
    gx_ref,
    gy_ref,
    cu_ref,
    d_ref,
    acc_ref,
):
    refs = (lo_ref, mid_ref, hi_ref)
    smalls = [[small_rows(refs[q], p) for p in range(3)] for q in range(3)]
    edges = [
        [(s[0:8] + s[8:16]) + s[16:24] if (p, q) != (1, 1) else None for p, s in enumerate(row)]
        for q, row in enumerate(smalls)
    ]
    edges[1][1] = tab_ref[...]
    blank = jnp.zeros((8, SPAN), F32)
    for c, regions in enumerate(CHUNKS):
        parts = []
        for big_a, big_b in regions:
            p = 0 if big_a == 0 else 2 if big_a == 4 else 1
            q = 0 if big_b == 0 else 2 if big_b == 4 else 1
            a = (2, big_a - 1, 0)[p]
            b = (2, big_b - 1, 0)[q]
            at = PLACE[a, b]
            parts.append(edges[q][p][:, at : at + SPAN])
        parts += [blank] * (4 - len(parts))
        chunk_ref[c] = jnp.concatenate(parts, axis=1)
    chunk_ref[7] = jnp.zeros((8, LANES), F32)
    rows = [chunk_ref[:, k, :] for k in range(8)]
    pos_x, pos_y, diff, vel_x, vel_y, rate, source, flag = rows
    spot = lax.broadcasted_iota(jnp.int32, (8, LANES), 0) * 4 + (
        lax.broadcasted_iota(jnp.int32, (8, LANES), 1) // SPAN
    )

    def among(test):
        hit = jnp.zeros((8, LANES), F32)
        for c, regions in enumerate(CHUNKS):
            for k, region in enumerate(regions):
                if test(region):
                    hit = jnp.where(spot == 4 * c + k, 1.0, hit)
        return hit

    off_x = among(lambda r: r[0] == 4) - among(lambda r: r[0] == 0)
    off_y = among(lambda r: r[1] == 4) - among(lambda r: r[1] == 0)
    own = (1.0 - off_x * off_x) * (1.0 - off_y * off_y) * flag
    wide_x = DELTA + (1.0 - 3.0 * DELTA) * among(lambda r: r[0] == 2)
    wide_y = DELTA + (1.0 - 3.0 * DELTA) * among(lambda r: r[1] == 2)
    area = wide_x * wide_y / SPAN * flag
    coords_x = [pos_x + (off_x - float(p)) for p in (-1, 0, 1)]
    coords_y = [pos_y + (off_y - float(q)) for q in (-1, 0, 1)]
    bumps_x = [bump(t) for t in coords_x]
    bumps_y = [bump(s) for s in coords_y]
    for q in range(3):
        for p in range(3):
            present = smalls[q][p][29:30, 0:LANES]
            b_x, b_y = bumps_x[p], bumps_y[q]
            window = b_x[0] * b_y[0] * present
            window_x = b_x[1] * b_y[0] * present
            window_y = b_x[0] * b_y[1] * present
            window_l = (b_x[2] * b_y[0] + b_x[0] * b_y[2]) * present
            n = 3 * q + p
            coef_ref[n, 0] = 2.0 * coords_x[p] - 1.0
            coef_ref[n, 1] = 2.0 * coords_y[q] - 1.0
            coef_ref[n, 2] = (
                -diff * window_l + vel_x * window_x + vel_y * window_y - rate * window
            )
            coef_ref[n, 3] = -2.0 * diff * window_x + vel_x * window
            coef_ref[n, 4] = -2.0 * diff * window_y + vel_y * window
            coef_ref[n, 5] = -diff * window
            col_ref[n] = columns_of(smalls[q][p])
    total_ref[...] = jnp.zeros((8, LANES), F32)

    def coefs(n, c):
        return [coef_ref[n, k, pl.ds(c, 1), :] for k in range(6)]

    def add_field(c, mix, cols):
        total_ref[pl.ds(c, 1), :] += jnp.sum(mix * cols[:, 7:8], axis=0, keepdims=True)

    def sweep(q, places, chunks):
        def step(i, carry):
            p = select(i, places)
            c = select(i, chunks)
            xi, eta, *cs = coefs(3 * q + p, c)
            cols = col_ref[3 * q + p]
            _, _, h2, gx, gy, curve = forward(cols, refs[q][p, 0:H, :], xi, eta)
            add_field(c, output_mix(cs, h2, gx, gy, curve), cols)
            return carry

        lax.fori_loop(0, len(places), step, 0)

    def own_step(c, carry):
        xi, eta, *cs = coefs(4, c)
        cols = col_ref[4]
        h1, streams, h2, gx, gy, curve = forward(cols, mid_ref[1, 0:H, :], xi, eta)
        h1_ref[c] = h1
        s_ref[c] = streams
        h2_ref[c] = h2
        gx_ref[c] = gx
        gy_ref[c] = gy
        cu_ref[c] = curve
        add_field(c, output_mix(cs, h2, gx, gy, curve), cols)
        return carry

    lax.fori_loop(0, 7, own_step, 0)
    sweep(1, (0, 0, 0, 2, 2, 2), (0, 1, 4, 2, 3, 4))
    sweep(0, (0, 1, 1, 1, 2), (0, 0, 2, 5, 2))
    sweep(2, (0, 1, 1, 1, 2), (1, 1, 3, 5, 3))

    residual = total_ref[...] - source
    loss = jnp.sum(own * area * residual * residual)
    total_ref[...] = 2.0 * area * residual
    acc_ref[...] = jnp.zeros(acc_ref.shape, F32)
    gw_ref[...] = jnp.zeros((H, H), F32)

    def back_step(c, carry):
        xi, eta, *cs = coefs(4, c)
        cols = col_ref[4]
        adjoint = total_ref[pl.ds(c, 1), :]
        c0, c1, c2, c3 = (adjoint * k for k in cs)
        h1, h2, gx, gy, curve = h1_ref[c], h2_ref[c], gx_ref[c], gy_ref[c], cu_ref[c]
        acc_ref[4] += output_mix((c0, c1, c2, c3), h2, gx, gy, curve)
        head = cols[:, 7:8]
        d2 = 1.0 - h2 * h2
        square = gx * gx + gy * gy
        e0, e1, e2, e3 = c0 * head, c1 * head, c2 * head, c3 * head
        d_damp = e1 * gx + e2 * gy + (curve - 2.0 * h2 * square) * e3
        d_hid = e0 - 2.0 * d2 * square * e3 - 2.0 * h2 * d_damp
        d_base = d_hid * d2
        turn = 4.0 * h2 * d2 * e3
        acc_ref[3] += d_base
        d_ref[:, 0:LANES] = d_base.astype(BF16)
        d_ref[:, LANES : 2 * LANES] = (e1 * d2 - turn * gx).astype(BF16)
        d_ref[:, 2 * LANES : 3 * LANES] = (e2 * d2 - turn * gy).astype(BF16)
        d_ref[:, 3 * LANES :] = (d2 * e3).astype(BF16)
        d_mixed = d_ref[...]
        gw_ref[...] += lax.dot_general(
            s_ref[c], d_mixed, (((1,), (1,)), ((), ())), preferred_element_type=F32
        )
        d_streams = jnp.dot(w_ref[0, 0], d_mixed, preferred_element_type=F32)
        ds0 = d_streams[:, 0:LANES]
        ds1 = d_streams[:, LANES : 2 * LANES]
        ds2 = d_streams[:, 2 * LANES : 3 * LANES]
        ds3 = d_streams[:, 3 * LANES :]
        w1, w2, w1x2, w2x2, pw = (cols[:, k : k + 1] for k in (0, 1, 3, 4, 5))
        d1 = 1.0 - h1 * h1
        d_damp1 = w1x2 * ds1 + w2x2 * ds2 + h1 * pw * ds3
        d_hid1 = ds0 + d1 * pw * ds3 - 2.0 * h1 * d_damp1
        d_pre = d_hid1 * d1
        turn1 = 8.0 * h1 * ds3
        acc_ref[0] += 2.0 * d1 * (ds1 - turn1 * w1) + xi * d_pre
        acc_ref[1] += 2.0 * d1 * (ds2 - turn1 * w2) + eta * d_pre
        acc_ref[2] += d_pre
        return carry

    lax.fori_loop(0, 7, back_step, 0)
    sums = [jnp.sum(acc_ref[k], axis=1, keepdims=True) for k in range(5)]
    grid = jnp.concatenate(sums + [jnp.zeros((H, 3), F32)], axis=1)
    gs = jnp.transpose(grid)
    gs_ref[...] = gs
    gw = gw_ref[...]
    square = jnp.sum(gw * gw) + jnp.sum(gs * gs)
    lane = lax.broadcasted_iota(jnp.int32, stat_ref.shape, 2)
    stat_ref[...] = jnp.where(lane == 0, square, jnp.where(lane == 1, loss, 0.0))


def sum_kernel(got_ref, out_ref):
    total = jnp.sum(got_ref[...], axis=0, keepdims=True)
    out_ref[...] = jnp.broadcast_to(total, out_ref.shape)


def scale_kernel(nets, got_ref, gw_ref, gs_ref, o0, o1, o2, o3, o4, loss_ref):
    total = jnp.sum(got_ref[...], axis=0)
    rms = jnp.sqrt(total[:, 0:1] / (nets * (H * H + 5 * H)) + EPS)
    gs = gs_ref[...] / rms
    o0[0, 0] = gs[0:2]
    o1[0] = gs[2:3]
    o2[0, 0] = gw_ref[...] / rms
    o3[0] = gs[3:4]
    o4[0] = gs[4:5]
    loss_ref[...] = total[:, 1:2]


def call(kernel, outs, scratch=(), limit=16 << 20):
    return pl.pallas_call(
        kernel,
        out_shape=outs,
        scratch_shapes=scratch,
        compiler_params=pltpu.CompilerParams(vmem_limit_bytes=limit),
    )


def shape(dims, kind=F32):
    return jax.ShapeDtypeStruct(dims, kind)


GX = ("z", "yh", "c")
GY = ("yl", "x")
FIRST = ("z", "c")
SECOND = ("yh", "yl", "x")


def local(
    points,
    diffusion,
    drift,
    ionization,
    source,
    in_weight,
    in_bias,
    mid_weight,
    mid_bias,
    out_weight,
):
    count_x = lax.axis_size(GX)
    count_y = lax.axis_size(GY)
    payload, table = call(pack_kernel, (shape((ROWS, H), BF16), shape((8, 384))))(
        points,
        diffusion,
        drift,
        ionization,
        source,
        in_weight,
        in_bias,
        mid_weight,
        mid_bias,
        out_weight,
    )
    forth = [(i, i + 1) for i in range(count_x - 1)]
    back = [(i + 1, i) for i in range(count_x - 1)]
    before = lax.ppermute(payload, GX, forth)
    after = lax.ppermute(payload, GX, back)
    row = jnp.stack([before, payload, after])
    ring = [(i, (i + 1) % count_y) for i in range(count_y)]
    below = lax.ppermute(row, GY, ring)
    above = lax.ppermute(row, GY, [(j, i) for i, j in ring])
    first = lax.axis_size(FIRST)
    second = lax.axis_size(SECOND)
    state = pltpu.VMEM((7, H, LANES), F32)
    grad_w, grad_s, stat = call(
        net_kernel,
        (shape((H, H)), shape((8, H)), shape((first, 1, LANES))),
        (
            pltpu.VMEM((8, 8, LANES), F32),
            pltpu.VMEM((9, 6, 8, LANES), F32),
            pltpu.VMEM((8, LANES), F32),
            pltpu.VMEM((9, H, 8), F32),
            state,
            pltpu.VMEM((7, H, 4 * LANES), BF16),
            state,
            state,
            state,
            state,
            pltpu.VMEM((H, 4 * LANES), BF16),
            pltpu.VMEM((5, H, LANES), F32),
        ),
        limit=32 << 20,
    )(row, below, above, table, mid_weight)
    got = lax.all_to_all(stat, FIRST, 0, 0, tiled=True)
    part = call(sum_kernel, shape((second, 1, LANES)))(got)
    got = lax.all_to_all(part, SECOND, 0, 0, tiled=True)
    outs = call(
        lambda *refs: scale_kernel(count_x * count_y, *refs),
        (
            shape((1, 1, 2, H)),
            shape((1, 1, H)),
            shape((1, 1, H, H)),
            shape((1, 1, H)),
            shape((1, 1, H)),
            shape((1, 1)),
        ),
    )(got, grad_w, grad_s)
    return (*outs[:5], outs[5].reshape(()))


def solution(mesh):
    fine = Mesh(
        mesh.devices.reshape(8, 2, 2, 4, 4), ("z", "yh", "c", "yl", "x")
    )
    return jax.shard_map(
        local,
        mesh=fine,
        in_specs=(
            P(None, GX, GY, None),
            P(GX, GY, None),
            P(None, GX, GY, None),
            P(GX, GY, None),
            P(GX, GY, None),
            P(GX, GY, None, None),
            P(GX, GY, None),
            P(GX, GY, None, None),
            P(GX, GY, None),
            P(GX, GY, None),
        ),
        out_specs=(
            P(GX, GY, None, None),
            P(GX, GY, None),
            P(GX, GY, None, None),
            P(GX, GY, None),
            P(GX, GY, None),
            P(),
        ),
        check_vma=False,
    )
```

time: 368 us -> 91.9 us (0.25)
  matrix products: 80.2 us -> 0 us
  blocking collectives: 107 us -> 37.4 us
  other arithmetic: 69.3 us -> 0.05 us
  local copies, waits for them, and re-layouts: 37.8 us -> 2.33 us
  starting transfers between devices: 40 us -> 18.6 us
  Pallas kernels: 0 us -> 18.1 us
  between operations: 9.29 us -> 0.76 us
  waiting for transfers between devices: 20.6 us -> 14.1 us
    psum x1 -> x0, blocking collectives: 107 us -> none  [local(): square = lax.psum(square_local, ('gx', 'gy'))]
    dot_general x99 -> x0, matrix products: 80.2 us -> none  [the longest x27 26.7 us: net_backward(): jnp.dot(cots[index], outputs[index], precision=lax.Precision.HIGHEST)]
    all_to_all x0 -> x2, blocking collectives: none -> 37.4 us  [the longest x1 24.6 us: local(): got = lax.all_to_all(stat, FIRST, 0, 0, tiled=True)]
    reduce_sum x22 -> x0, other arithmetic: 22 us -> none  [the longest x9 13.9 us: net_backward(): d_bmid = jnp.sum(d_base, axis=0)]
    ppermute x8 -> x4, starting transfers between devices: 40 us -> 18.6 us  [the longest x1 8.79 us: local(): after = lax.ppermute(payload, GX, back)]
    pallas_call x0 -> x4, Pallas kernels: none -> 18.1 us  [the longest x1 17.1 us: local(): call(net_kernel, (shape((H, H)), shape((8, H)), shape((first, 1, LANES)))...]
    mul x19 -> x0, other arithmetic: 12.7 us -> none  [the longest x9 5.91 us: net_backward(): 8.0 * damp_one * power * ds_three]
    convert_element_type x12 -> x0, other arithmetic: 8.74 us -> none  [the longest x9 6.62 us: net_fields(): head = params[4].astype(jnp.float32)]
  transfers between devices with their start and end apart: 8 -> 4, of which waited for: 3 -> 4; matrix products, arithmetic and copies ran while one was open for 16% -> 0% of each run, Pallas kernels for 0% -> 0%
where the time goes in v1:
time: 91.9 us; the launch traced here: 91.4 us
  blocking collectives  37.4 us (41%)
  starting transfers between devices  18.6 us (20%)
  Pallas kernels  18.1 us (20%)
  waiting for transfers between devices  14.1 us (15%)
  local copies, waits for them, and re-layouts  2.33 us (3%)
    all_to_all x1, blocking collectives, local(): got = lax.all_to_all(stat, FIRST, 0, 0, tiled=True)  24.6 us
    pallas_call x1, Pallas kernels, local(): call(net_kernel, (shape((H, H)), shape((8, H)), shape((first, 1, LANES)))...  17.1 us
    all_to_all x1, blocking collectives, local(): got = lax.all_to_all(part, SECOND, 0, 0, tiled=True)  12.8 us
    ppermute x1, starting transfers between devices, local(): after = lax.ppermute(payload, GX, back)  8.79 us
    ppermute x1, waiting for transfers between devices, local(): below = lax.ppermute(row, GY, ring)  6.03 us
    ppermute x1, starting transfers between devices, local(): above = lax.ppermute(row, GY, [(j, i) for i, j in ring])  5.96 us
    ppermute x1, waiting for transfers between devices, local(): above = lax.ppermute(row, GY, [(j, i) for i, j in ring])  4.99 us
    unnamed x22, local copies, waits for them, and re-layouts  2.33 us
  transfers between devices with their start and end apart: 4, of which 4 were waited for; matrix products, arithmetic and copies ran while one was open for 0% of the time, Pallas kernels for 0%

profile of v1, /device:TPU:1, one launch (start us, length us, event | category | flops | bytes accessed | tf_op | source)
XLA Modules:
  0.0 91.4 jit_solution(15946116388830985014)
XLA Ops:
  0.7 0.7 copy.16.pts
  1.4 0.0 copy-start.4
  1.4 0.0 copy-start.5
  1.4 0.0 copy-start.6
  1.5 0.6 copy-done.2
  2.1 0.0 copy-done.3
  2.1 0.0 copy-done.4
  2.1 0.0 copy-done.6
  2.1 0.0 copy-done.7
  2.1 0.9 copy-done
  3.0 0.1 shard_map.145
  3.2 8.8 %collective-permute-start.1 = (bf16[288,256]{1,0:T(8,128)(2,1)S(1)}, bf16[288,256]{1,0:T(8,128)(2,1)S(1)}, u32[]{:S(2)}, u32[]{:S(2)}) collective-permute-start(bf16[288,256]{1,0:T(8,128)(2,1)S(1)} %get-tuple-element.17), channel_id=1, source_target_pairs={{16,0},{32,16},{48,32},{64,48},{80,64},{96,80},{112,96},{128,112},... | collective-permute-start | bytes 442376 | tf_op jit(solution)/shard_map/ppermute | solution.py:401
  12.0 2.0 %collective-permute-start = (bf16[288,256]{1,0:T(8,128)(2,1)S(1)}, bf16[288,256]{1,0:T(8,128)(2,1)S(1)}, u32[]{:S(2)}, u32[]{:S(2)}) collective-permute-start(bf16[288,256]{1,0:T(8,128)(2,1)S(1)} %get-tuple-element.17), channel_id=1, source_target_pairs={{0,16},{16,32},{32,48},{48,64},{64,80},{80,96},{96,112},{112,128},... | collective-permute-start | bytes 442376 | tf_op jit(solution)/shard_map/ppermute | solution.py:400
  14.0 1.0 %collective-permute-done.1 = bf16[288,256]{1,0:T(8,128)(2,1)S(1)} collective-permute-done((bf16[288,256]{1,0:T(8,128)(2,1)S(1)}, bf16[288,256]{1,0:T(8,128)(2,1)S(1)}, u32[]{:S(2)}, u32[]{:S(2)}) %collective-permute-start.1) | collective-permute-done | bytes 147488 | tf_op jit(solution)/shard_map/ppermute | solution.py:401
  14.9 2.1 %collective-permute-done = bf16[288,256]{1,0:T(8,128)(2,1)S(1)} collective-permute-done((bf16[288,256]{1,0:T(8,128)(2,1)S(1)}, bf16[288,256]{1,0:T(8,128)(2,1)S(1)}, u32[]{:S(2)}, u32[]{:S(2)}) %collective-permute-start) | collective-permute-done | bytes 147488 | tf_op jit(solution)/shard_map/ppermute | solution.py:400
  17.0 0.1 pad_maximum_fusion.mid_ref
  17.1 6.0 %collective-permute-start.3 = (bf16[3,288,256]{2,1,0:T(8,128)(2,1)S(1)}, bf16[3,288,256]{2,1,0:T(8,128)(2,1)S(1)}, u32[]{:S(2)}, u32[]{:S(2)}) collective-permute-start(bf16[3,288,256]{2,1,0:T(8,128)(2,1)S(1)} %pad_maximum_fusion.mid_ref), channel_id=1, source_target_pairs={{1,0},{2,1},{3,2},{4,3},{5,4},{6,5},{7,6},{8,7},{9,8},{10,9},{11,1... | collective-permute-start | bytes 1327112 | tf_op jit(solution)/shard_map/ppermute | solution.py:405
  23.1 1.9 %collective-permute-start.2 = (bf16[3,288,256]{2,1,0:T(8,128)(2,1)S(1)}, bf16[3,288,256]{2,1,0:T(8,128)(2,1)S(1)}, u32[]{:S(2)}, u32[]{:S(2)}) collective-permute-start(bf16[3,288,256]{2,1,0:T(8,128)(2,1)S(1)} %pad_maximum_fusion.mid_ref), channel_id=1, source_target_pairs={{0,1},{1,2},{2,3},{3,4},{4,5},{5,6},{6,7},{7,8},{8,9},{9,10},{10,1... | collective-permute-start | bytes 1327112 | tf_op jit(solution)/shard_map/ppermute | solution.py:404
  25.0 5.0 %collective-permute-done.3.hi_ref = bf16[3,288,256]{2,1,0:T(8,128)(2,1)S(1)} collective-permute-done((bf16[3,288,256]{2,1,0:T(8,128)(2,1)S(1)}, bf16[3,288,256]{2,1,0:T(8,128)(2,1)S(1)}, u32[]{:S(2)}, u32[]{:S(2)}) %collective-permute-start.3) | collective-permute-done | bytes 442400 | tf_op jit(solution)/shard_map/ppermute | solution.py:405
  30.0 6.0 %collective-permute-done.2.lo_ref = bf16[3,288,256]{2,1,0:T(8,128)(2,1)S(1)} collective-permute-done((bf16[3,288,256]{2,1,0:T(8,128)(2,1)S(1)}, bf16[3,288,256]{2,1,0:T(8,128)(2,1)S(1)}, u32[]{:S(2)}, u32[]{:S(2)}) %collective-permute-start.2) | collective-permute-done | bytes 442400 | tf_op jit(solution)/shard_map/ppermute | solution.py:404
  36.0 17.1 %shard_map.146 = (f32[256,256]{1,0:T(8,128)S(1)}, f32[8,256]{1,0:T(8,128)S(1)}, f32[16,1,128]{2,1,0:T(1,128)S(1)}) custom-call(bf16[3,288,256]{2,1,0:T(8,128)(2,1)S(1)} %pad_maximum_fusion.mid_ref, bf16[3,288,256]{2,1,0:T(8,128)(2,1)S(1)} %collective-permute-done.2.lo_ref, bf16[3,288,256]{2,1,0:T(8,128)(2,1)S(1)} %collective-permute-done.3.hi_ref, ...), custom_call_target="tpu_custom_call" | custom-call | tf_op jit(solution)/shard_map/pallas_call | solution.py:409
  53.2 24.6 %all_to_all.10.got_ref = f32[16,1,128]{2,1,0:T(1,128)S(1)} all-to-all(f32[16,1,128]{2,1,0:T(1,128)S(1)} %get-tuple-element.19), channel_id=1, replica_groups=mesh['z'=8,'yh'=2,'c'=2,'yl'=4,'x'=4] {'z','c'}, dimensions={0} | all-to-all | bytes 16384 | tf_op jit(solution)/shard_map/all_to_all | solution.py:428
  77.8 12.8 %all_to_all.11.refs_0_ = f32[32,1,128]{2,1,0:T(1,128)S(1)} all-to-all(f32[32,1,128]{2,1,0:T(1,128)S(1)} %shard_map.147), channel_id=1, replica_groups=mesh['z'=8,'yh'=2,'c'=2,'yl'=4,'x'=4] {'yh','yl','x'}, dimensions={0} | all-to-all | bytes 32768 | tf_op jit(solution)/shard_map/all_to_all | solution.py:430
  90.6 0.8 shard_map.148
  (13 shorter events, 0.1 us)
Async XLA Ops:
  0.6 0.7 copy-start.9
  0.6 0.8 copy-start.8
  1.4 0.7 copy-start.2
  1.4 0.7 copy-start.3
  1.4 0.7 copy-start.4
  1.4 0.7 copy-start.5
  1.4 0.7 copy-start.6
  1.4 0.7 copy-start.7
  2.1 0.9 copy-start
  3.2 11.8 %collective-permute-start.1 = (bf16[288,256]{1,0:T(8,128)(2,1)S(1)}, bf16[288,256]{1,0:T(8,128)(2,1)S(1)}, u32[]{:S(2)}, u32[]{:S(2)}) collective-permute-start(bf16[288,256]{1,0:T(8,128)(2,1)S(1)} %get-tuple-element.17), channel_id=1, source_target_pairs={{16,0},{32,16},{48,32},{64,48},{80,64},{96,80},{112,96},{128,112},... | collective-permute-start | bytes 442376 | tf_op jit(solution)/shard_map/ppermute | solution.py:401
  12.0 5.1 %collective-permute-start = (bf16[288,256]{1,0:T(8,128)(2,1)S(1)}, bf16[288,256]{1,0:T(8,128)(2,1)S(1)}, u32[]{:S(2)}, u32[]{:S(2)}) collective-permute-start(bf16[288,256]{1,0:T(8,128)(2,1)S(1)} %get-tuple-element.17), channel_id=1, source_target_pairs={{0,16},{16,32},{32,48},{48,64},{64,80},{80,96},{96,112},{112,128},... | collective-permute-start | bytes 442376 | tf_op jit(solution)/shard_map/ppermute | solution.py:400
  17.0 19.0 %copy-start.1 = (bf16[1,1,256,256]{3,2,1,0:T(8,128)(2,1)S(1)}, bf16[1,1,256,256]{3,2,1,0:T(8,128)(2,1)}, u32[]{:S(2)}) copy-start(bf16[1,1,256,256]{3,2,1,0:T(8,128)(2,1)} %w_ref.1) | copy-start | bytes 393220
  17.1 12.9 %collective-permute-start.3 = (bf16[3,288,256]{2,1,0:T(8,128)(2,1)S(1)}, bf16[3,288,256]{2,1,0:T(8,128)(2,1)S(1)}, u32[]{:S(2)}, u32[]{:S(2)}) collective-permute-start(bf16[3,288,256]{2,1,0:T(8,128)(2,1)S(1)} %pad_maximum_fusion.mid_ref), channel_id=1, source_target_pairs={{1,0},{2,1},{3,2},{4,3},{5,4},{6,5},{7,6},{8,7},{9,8},{10,9},{11,1... | collective-permute-start | bytes 1327112 | tf_op jit(solution)/shard_map/ppermute | solution.py:405
  23.1 13.0 %collective-permute-start.2 = (bf16[3,288,256]{2,1,0:T(8,128)(2,1)S(1)}, bf16[3,288,256]{2,1,0:T(8,128)(2,1)S(1)}, u32[]{:S(2)}, u32[]{:S(2)}) collective-permute-start(bf16[3,288,256]{2,1,0:T(8,128)(2,1)S(1)} %pad_maximum_fusion.mid_ref), channel_id=1, source_target_pairs={{0,1},{1,2},{2,3},{3,4},{4,5},{5,6},{6,7},{7,8},{8,9},{9,10},{10,1... | collective-permute-start | bytes 1327112 | tf_op jit(solution)/shard_map/ppermute | solution.py:404

commit v2 on v1

v2 whole, which is shorter than its diff:
```python
import jax
import jax.numpy as jnp
from jax import lax
from jax.experimental import pallas as pl
from jax.experimental.pallas import tpu as pltpu
from jax.sharding import Mesh, PartitionSpec as P

DELTA = 0.25
EPS = 1e-06
H = 256
LANES = 128
SPAN = 32
ROWS = 288
F32 = jnp.float32
BF16 = jnp.bfloat16

MIDDLE = (
    ((0, 1), (1, 1), (0, 3), (1, 3)),
    ((3, 1), (4, 1), (3, 3), (4, 3)),
    ((0, 2), (1, 2), (3, 2), (4, 2)),
    ((2, 1), (2, 2), (2, 3)),
)
HIGH = (
    ((0, 3), (0, 4), (1, 3), (1, 4)),
    ((3, 3), (3, 4), (4, 3), (4, 4)),
    ((2, 3), (2, 4)),
    ((0, 4), (1, 4), (3, 4), (4, 4)),
)
BELOW = (
    ((0, 0), (0, 1), (1, 0), (1, 1)),
    ((3, 0), (3, 1), (4, 0), (4, 1)),
    ((2, 0), (2, 1)),
    ((0, 0), (1, 0), (3, 0), (4, 0)),
    ((2, 0), (2, 4)),
)
WINDOW = MIDDLE + (HIGH[3], BELOW[3], BELOW[4])
PLACE = {
    (0, 0): 0,
    (0, 1): 32,
    (0, 2): 64,
    (1, 0): 96,
    (2, 0): 128,
    (2, 1): 160,
    (2, 2): 192,
    (1, 2): 224,
    (1, 1): 256,
}
LOW = (0.0, DELTA, 1.0 - DELTA)
WIDTH = (DELTA, 1.0 - 2.0 * DELTA, DELTA)


def smooth_rise(coord):
    ramp = jnp.clip((coord + DELTA) / (2.0 * DELTA), 0.0, 1.0)
    value = ramp * ramp * ramp * (10.0 - 15.0 * ramp + 6.0 * ramp * ramp)
    slope = 30.0 * ramp * ramp * (1.0 - ramp) * (1.0 - ramp) / (2.0 * DELTA)
    bend = 60.0 * ramp * (1.0 - ramp) * (1.0 - 2.0 * ramp) / (4.0 * DELTA * DELTA)
    return (value, slope, bend)


def bump(coord):
    rise_a = smooth_rise(coord)
    rise_b = smooth_rise(coord - 1.0)
    return (rise_a[0] - rise_b[0], rise_a[1] - rise_b[1], rise_a[2] - rise_b[2])


def pack_kernel(*refs):
    sources, (pay_ref, tab_ref), buffers, sems = (
        refs[:10],
        refs[10:12],
        refs[12:22],
        refs[22],
    )
    pts, dif, dri, ion, src, w_in, b_in, w_mid, b_mid, w_out = buffers
    strips = [pl.ds(64 * k, 64) for k in range(4)]
    pairs = [(sources[7].at[0, 0, k], w_mid.at[0, 0, k]) for k in strips]
    pairs += [(sources[k], buffers[k]) for k in range(10) if k != 7]
    copies = [
        pltpu.make_async_copy(one, two, sems.at[k]) for k, (one, two) in enumerate(pairs)
    ]
    for copy in copies:
        copy.start()
    for copy in copies[4:]:
        copy.wait()
    zeros = jnp.zeros((1, SPAN), F32)
    ones = jnp.ones((1, SPAN), F32)
    pieces = {}
    for a in range(3):
        for b in range(3):
            rows = [
                LOW[a] + WIDTH[a] * pts[a, b, 0:1, :],
                LOW[b] + WIDTH[b] * pts[a, b, 1:2, :],
                dif[a, b : b + 1, :],
                dri[a, b, 0:1, :],
                dri[a, b, 1:2, :],
                ion[a, b : b + 1, :],
                src[a, b : b + 1, :],
                ones,
            ]
            pieces[PLACE[a, b]] = jnp.concatenate(rows, axis=0)
    blank = jnp.concatenate([zeros] * 8, axis=0)
    order = [pieces.get(32 * k, blank) for k in range(12)]
    tabs = [jnp.concatenate(order[4 * k : 4 * k + 4], axis=1) for k in range(3)]
    for k in range(3):
        tab_ref[:, 128 * k : 128 * k + 128] = tabs[k]
    edge = jnp.concatenate(tabs[:2], axis=1)
    high = edge.astype(BF16).astype(F32)
    rest = edge - high
    mid = rest.astype(BF16).astype(F32)
    low = rest - mid
    small = jnp.concatenate(
        [
            w_in[0, 0].astype(F32),
            b_in[0].astype(F32),
            b_mid[0].astype(F32),
            w_out[0].astype(F32),
            jnp.ones((1, H), F32),
            jnp.zeros((2, H), F32),
        ],
        axis=0,
    )
    pay_ref[H:ROWS, :] = jnp.concatenate([high, mid, low, small], axis=0).astype(BF16)
    for copy in copies[:4]:
        copy.wait()
    pay_ref[0:H, :] = jnp.transpose(w_mid[0, 0].astype(F32)).astype(BF16)


def small_rows(ref):
    return [ref[p, H:ROWS, :].astype(F32) for p in range(3)]


def tables(smalls):
    return [(s[0:8] + s[8:16]) + s[16:24] for s in smalls]


def gather_rows(chunk_ref, layout, points):
    blank = jnp.zeros((8, SPAN), F32)
    for c, regions in enumerate(layout):
        parts = []
        for big_a, big_b in regions:
            p = 0 if big_a == 0 else 2 if big_a == 4 else 1
            q = 0 if big_b == 0 else 2 if big_b == 4 else 1
            at = PLACE[(2, big_a - 1, 0)[p], (2, big_b - 1, 0)[q]]
            parts.append(points[q][p][:, at : at + SPAN])
        parts += [blank] * (4 - len(parts))
        chunk_ref[c] = jnp.concatenate(parts, axis=1)
    for c in range(len(layout), 8):
        chunk_ref[c] = jnp.zeros((8, LANES), F32)
    return [chunk_ref[:, k, :] for k in range(8)]


def frame(layout, flag):
    spot = lax.broadcasted_iota(jnp.int32, (8, LANES), 0) * 4 + (
        lax.broadcasted_iota(jnp.int32, (8, LANES), 1) // SPAN
    )

    def among(test):
        hit = jnp.zeros((8, LANES), F32)
        for c, regions in enumerate(layout):
            for k, region in enumerate(regions):
                if test(region):
                    hit = jnp.where(spot == 4 * c + k, 1.0, hit)
        return hit

    off_x = among(lambda r: r[0] == 4) - among(lambda r: r[0] == 0)
    off_y = among(lambda r: r[1] == 4) - among(lambda r: r[1] == 0)
    own = (1.0 - off_x * off_x) * (1.0 - off_y * off_y)
    wide_x = DELTA + (1.0 - 3.0 * DELTA) * among(lambda r: r[0] == 2)
    wide_y = DELTA + (1.0 - 3.0 * DELTA) * among(lambda r: r[1] == 2)
    return off_x, off_y, wide_x * wide_y / SPAN * flag, own


def put_coefs(coef_ref, rows, off_x, off_y, nets):
    pos_x, pos_y, diff, vel_x, vel_y, rate = rows[:6]
    coords_x = {p: pos_x + (off_x - float(p)) for p, _, _ in nets}
    coords_y = {q: pos_y + (off_y - float(q)) for _, q, _ in nets}
    bumps_x = {p: bump(t) for p, t in coords_x.items()}
    bumps_y = {q: bump(s) for q, s in coords_y.items()}
    for n, (p, q, present) in enumerate(nets):
        b_x, b_y = bumps_x[p], bumps_y[q]
        window = b_x[0] * b_y[0] * present
        window_x = b_x[1] * b_y[0] * present
        window_y = b_x[0] * b_y[1] * present
        window_l = (b_x[2] * b_y[0] + b_x[0] * b_y[2]) * present
        coef_ref[n, 0] = 2.0 * coords_x[p] - 1.0
        coef_ref[n, 1] = 2.0 * coords_y[q] - 1.0
        coef_ref[n, 2] = (
            -diff * window_l + vel_x * window_x + vel_y * window_y - rate * window
        )
        coef_ref[n, 3] = -2.0 * diff * window_x + vel_x * window
        coef_ref[n, 4] = -2.0 * diff * window_y + vel_y * window
        coef_ref[n, 5] = -diff * window


def spread(smalls, par_ref):
    lane = lax.broadcasted_iota(jnp.int32, (8, 5 * LANES), 1) // LANES
    line = lax.broadcasted_iota(jnp.int32, (8, 5 * LANES), 0)
    pick = jnp.where(lane == line, 1.0, 0.0).astype(BF16)
    for n, small in enumerate(smalls):
        wide = lax.dot_general(
            small[24:32].astype(BF16),
            pick,
            (((0,), (0,)), ((), ())),
            preferred_element_type=F32,
        )
        for k in range(5):
            par_ref[n, k] = wide[:, LANES * k : LANES * k + LANES]
        w_first, w_second = wide[:, 0:LANES], wide[:, LANES : 2 * LANES]
        par_ref[n, 5] = -8.0 * (w_first * w_first + w_second * w_second)


def forward(par_ref, n, weights, xi, eta):
    w_first, w_second = par_ref[n, 0], par_ref[n, 1]
    h1 = jnp.tanh(xi * w_first + eta * w_second + par_ref[n, 2])
    d1 = 1.0 - h1 * h1
    d1x2 = 2.0 * d1
    streams = jnp.concatenate(
        [
            h1.astype(BF16),
            (d1x2 * w_first).astype(BF16),
            (d1x2 * w_second).astype(BF16),
            (h1 * d1 * par_ref[n, 5]).astype(BF16),
        ],
        axis=1,
    )
    mixed = jnp.dot(weights, streams, preferred_element_type=F32)
    h2 = jnp.tanh(mixed[:, 0:LANES] + par_ref[n, 3])
    gx = mixed[:, LANES : 2 * LANES]
    gy = mixed[:, 2 * LANES : 3 * LANES]
    curve = mixed[:, 3 * LANES :]
    return h1, streams, h2, gx, gy, curve


def coefs(coef_ref, n, c):
    return [coef_ref[n, k, c : c + 1, :] for k in range(6)]


def add_field(total_ref, c, mix, head):
    total_ref[c : c + 1, :] += jnp.sum(mix * head, axis=0, keepdims=True)


def near_step(total_ref, coef_ref, n, c, par_ref, m, weights):
    xi, eta, c0, c1, c2, c3 = coefs(coef_ref, n, c)
    _, _, h2, gx, gy, curve = forward(par_ref, m, weights, xi, eta)
    d2 = 1.0 - h2 * h2
    square = gx * gx + gy * gy
    inner = c1 * gx + c2 * gy + c3 * (curve - 2.0 * h2 * square)
    add_field(total_ref, c, c0 * h2 + d2 * inner, par_ref[m, 4])


def own_step(total_ref, coef_ref, n, c, par_ref, weights, k, s_ref, state_ref):
    xi, eta, c0, c1, c2, c3 = coefs(coef_ref, n, c)
    h1, streams, h2, gx, gy, curve = forward(par_ref, 1, weights, xi, eta)
    d2 = 1.0 - h2 * h2
    square = gx * gx + gy * gy
    inner = c1 * gx + c2 * gy + c3 * (curve - 2.0 * h2 * square)
    mix = c0 * h2 + d2 * inner
    head = par_ref[1, 4]
    add_field(total_ref, c, mix, head)
    turn = (4.0 * c3) * h2
    s_ref[k] = streams
    state_ref[k, 0] = h1
    state_ref[k, 1] = mix
    state_ref[k, 2] = head * d2
    state_ref[k, 3] = c0 - 2.0 * (d2 * square * c3 + h2 * inner)
    state_ref[k, 4] = c1 - turn * gx
    state_ref[k, 5] = c2 - turn * gy


def middle_kernel(
    mid_ref, tab_ref, par_ref, coef_ref, info_ref, s_ref, state_ref, chunk_ref, total_ref
):
    smalls = small_rows(mid_ref)
    points = tables(smalls)
    points[1] = tab_ref[...]
    rows = gather_rows(chunk_ref, MIDDLE, [None, points, None])
    off_x, off_y, area, own = frame(MIDDLE, rows[7])
    nets = [(p - 1, 0, smalls[p][29:30, 0:LANES]) for p in range(3)]
    put_coefs(coef_ref, rows, off_x, off_y, nets)
    spread(smalls, par_ref)
    total_ref[...] = jnp.zeros((8, LANES), F32)
    for c in range(4):
        own_step(
            total_ref, coef_ref, 1, c, par_ref, mid_ref[1, 0:H, :], c, s_ref, state_ref
        )
    for p, c in ((0, 0), (2, 1), (0, 2), (2, 2)):
        near_step(total_ref, coef_ref, p, c, par_ref, p, mid_ref[p, 0:H, :])
    info_ref[0] = total_ref[...]
    info_ref[1] = area
    info_ref[2] = rows[6]
    info_ref[3] = own


def side(layout, q, mid_ref, side_ref, other, par_ref, work):
    coef_ref, total_ref, side_par, chunk_ref, s_ref, state_ref = work
    smalls = small_rows(mid_ref)
    far = small_rows(side_ref)
    points = [None, tables(smalls), None]
    points[1 + q] = tables(far)
    if other is not None:
        points[1 - q] = tables(small_rows(other))
    rows = gather_rows(chunk_ref, layout, points)
    off_x, off_y, area, _ = frame(layout, rows[7])
    nets = [(p - 1, 0, smalls[p][29:30, 0:LANES]) for p in range(3)]
    nets += [(p - 1, q, far[p][29:30, 0:LANES]) for p in range(3)]
    put_coefs(coef_ref, rows, off_x, off_y, nets)
    spread(far, side_par)
    total_ref[...] = jnp.zeros((8, LANES), F32)
    for k, c in enumerate(range(3, len(layout))):
        own_step(
            total_ref, coef_ref, 1, c, par_ref, mid_ref[1, 0:H, :], k, s_ref, state_ref
        )
    for p in (0, 2):
        near_step(total_ref, coef_ref, p, 3, par_ref, p, mid_ref[p, 0:H, :])
    for p, c in ((0, 0), (1, 0), (1, 1), (2, 1), (1, 2)):
        near_step(total_ref, coef_ref, 3 + p, c, side_par, p, side_ref[p, 0:H, :])
    return area, rows[6]


def high_kernel(
    mid_ref, hi_ref, par_ref, coef_ref, info_ref, s_ref, state_ref, side_par, chunk_ref, total_ref
):
    work = (coef_ref, total_ref, side_par, chunk_ref, s_ref, state_ref)
    area, source = side(HIGH, 1, mid_ref, hi_ref, None, par_ref, work)
    info_ref[0] = total_ref[...]
    info_ref[1] = area
    info_ref[2] = source


def moved(total, layout):
    places = {}
    for c, regions in enumerate(layout[:3]):
        for k, region in enumerate(regions):
            places[region] = (c, SPAN * k)
    rows = []
    for regions in WINDOW:
        parts = []
        for region in regions:
            if region in places:
                c, at = places[region]
                parts.append(total[c : c + 1, at : at + SPAN])
            else:
                parts.append(jnp.zeros((1, SPAN), F32))
        parts += [jnp.zeros((1, SPAN), F32)] * (4 - len(parts))
        rows.append(jnp.concatenate(parts, axis=1))
    return jnp.concatenate(rows + [jnp.zeros((1, LANES), F32)], axis=0)


def last_kernel(
    mid_ref,
    lo_ref,
    hi_ref,
    w_ref,
    par_ref,
    coef_m,
    info_m,
    s_m,
    state_m,
    coef_h,
    info_h,
    s_h,
    state_h,
    gw_ref,
    gs_ref,
    stat_ref,
    coef_l,
    s_l,
    state_l,
    side_par,
    chunk_ref,
    total_ref,
    d_ref,
    acc_ref,
):
    work = (coef_l, total_ref, side_par, chunk_ref, s_l, state_l)
    area_l, source_l = side(BELOW, -1, mid_ref, lo_ref, hi_ref, par_ref, work)
    below = total_ref[...]
    high = info_h[0]

    def joined(m, h, l):
        return jnp.concatenate(
            [m[0:4], h[3:4], l[3:5], jnp.zeros((1, LANES), F32)], axis=0
        )

    area = joined(info_m[1], info_h[1], area_l)
    source = joined(info_m[2], info_h[2], source_l)
    total = joined(info_m[0], high, below) + moved(high, HIGH) + moved(below, BELOW)
    residual = total - source
    line = lax.broadcasted_iota(jnp.int32, (8, LANES), 0)
    own = jnp.where(line < 4, info_m[3], 0.0)
    loss = jnp.sum(own * area * residual * residual)
    total_ref[...] = 2.0 * area * residual
    acc_ref[...] = jnp.zeros(acc_ref.shape, F32)
    gw_ref[...] = jnp.zeros((H, H), F32)
    w1, w2, pw = par_ref.at[1, 0], par_ref.at[1, 1], par_ref.at[1, 5]
    places = [(coef_m, c, s_m, state_m, c) for c in range(4)]
    places += [(coef_h, 3, s_h, state_h, 0), (coef_l, 3, s_l, state_l, 0)]
    places += [(coef_l, 4, s_l, state_l, 1)]
    for row, (coef_ref, c, s_ref, state_ref, k) in enumerate(places):
        xi, eta, _, _, _, c3 = coefs(coef_ref, 1, c)
        adjoint = total_ref[row : row + 1, :]
        h1 = state_ref[k, 0]
        scale = state_ref[k, 2] * adjoint
        d_base = scale * state_ref[k, 3]
        acc_ref[5] += state_ref[k, 1] * adjoint
        acc_ref[4] += d_base
        d_ref[row % 2, :, 0:LANES] = d_base.astype(BF16)
        d_ref[row % 2, :, LANES : 2 * LANES] = (scale * state_ref[k, 4]).astype(BF16)
        d_ref[row % 2, :, 2 * LANES : 3 * LANES] = (scale * state_ref[k, 5]).astype(BF16)
        d_ref[row % 2, :, 3 * LANES :] = (scale * c3).astype(BF16)
        d_mixed = d_ref[row % 2]
        d_streams = jnp.dot(w_ref[0, 0], d_mixed, preferred_element_type=F32)
        gw_ref[...] += lax.dot_general(
            s_ref[k], d_mixed, (((1,), (1,)), ((), ())), preferred_element_type=F32
        )
        ds0 = d_streams[:, 0:LANES]
        ds1 = d_streams[:, LANES : 2 * LANES]
        ds2 = d_streams[:, 2 * LANES : 3 * LANES]
        ds3 = d_streams[:, 3 * LANES :]
        d1 = 1.0 - h1 * h1
        cross = w1[...] * ds1 + w2[...] * ds2
        d_pre = d1 * (ds0 + pw[...] * ds3 * (3.0 * d1 - 2.0) - (4.0 * h1) * cross)
        d1x2 = 2.0 * d1
        acc_ref[0] += d1x2 * ds1 + xi * d_pre
        acc_ref[1] += d1x2 * ds2 + eta * d_pre
        acc_ref[2] += d_pre
        acc_ref[3] += h1 * d1 * ds3
    sums = [jnp.sum(acc_ref[k], axis=1, keepdims=True) for k in range(6)]
    turn = -16.0 * sums[3]
    grid = jnp.concatenate(
        [
            sums[0] + turn * w1[:, 0:1],
            sums[1] + turn * w2[:, 0:1],
            sums[2],
            sums[4],
            sums[5],
            jnp.zeros((H, 3), F32),
        ],
        axis=1,
    )
    gs = jnp.transpose(grid)
    gs_ref[...] = gs
    gw = gw_ref[...]
    square = jnp.sum(gw * gw) + jnp.sum(gs * gs)
    lane = lax.broadcasted_iota(jnp.int32, stat_ref.shape, 2)
    stat_ref[...] = jnp.where(lane == 0, square, jnp.where(lane == 1, loss, 0.0))


def sum_kernel(got_ref, out_ref):
    total = jnp.sum(got_ref[...], axis=0, keepdims=True)
    out_ref[...] = jnp.broadcast_to(total, out_ref.shape)


def scale_kernel(nets, got_ref, gw_ref, gs_ref, o0, o1, o2, o3, o4, loss_ref):
    total = jnp.sum(got_ref[...], axis=0)
    rms = jnp.sqrt(total[:, 0:1] / (nets * (H * H + 5 * H)) + EPS)
    gs = gs_ref[...] / rms
    o0[0, 0] = gs[0:2]
    o1[0] = gs[2:3]
    o2[0, 0] = gw_ref[...] / rms
    o3[0] = gs[3:4]
    o4[0] = gs[4:5]
    loss_ref[...] = total[:, 1:2]


def call(kernel, outs, scratch=(), limit=16 << 20, flops=0, place=pltpu.VMEM):
    extra = {}
    if place != pltpu.VMEM:
        extra["in_specs"] = [pl.BlockSpec(memory_space=place)] * 10
    return pl.pallas_call(
        kernel,
        out_shape=outs,
        scratch_shapes=scratch,
        compiler_params=pltpu.CompilerParams(vmem_limit_bytes=limit),
        cost_estimate=pl.CostEstimate(
            flops=flops, bytes_accessed=1 << 18, transcendentals=0
        ),
        **extra,
    )


def shape(dims, kind=F32):
    return jax.ShapeDtypeStruct(dims, kind)


GX = ("z", "yh", "c")
GY = ("yl", "x")
FIRST = ("z", "c")
SECOND = ("yh", "yl", "x")


def local(
    points,
    diffusion,
    drift,
    ionization,
    source,
    in_weight,
    in_bias,
    mid_weight,
    mid_bias,
    out_weight,
):
    count_x = lax.axis_size(GX)
    count_y = lax.axis_size(GY)
    inputs = (
        points.transpose(1, 2, 0, 3),
        diffusion,
        drift.transpose(1, 2, 0, 3),
        ionization,
        source,
        in_weight,
        in_bias,
        mid_weight,
        mid_bias,
        out_weight,
    )
    payload, table = call(
        pack_kernel,
        (shape((ROWS, H), BF16), shape((8, 384))),
        tuple(pltpu.VMEM(x.shape, x.dtype) for x in inputs)
        + (pltpu.SemaphoreType.DMA((13,)),),
        place=pl.ANY,
        limit=16 << 20,
    )(*(pltpu.with_memory_space_constraint(x, pltpu.HBM) for x in inputs))
    forth = [(i, i + 1) for i in range(count_x - 1)]
    back = [(i + 1, i) for i in range(count_x - 1)]
    before = lax.ppermute(payload, GX, forth)
    after = lax.ppermute(payload, GX, back)
    row = jnp.stack([before, payload, after])
    ring = [(i, (i + 1) % count_y) for i in range(count_y)]
    above = lax.ppermute(row, GY, [(j, i) for i, j in ring])
    below = lax.ppermute(row, GY, ring)
    first = lax.axis_size(FIRST)
    second = lax.axis_size(SECOND)

    def kept(chunks):
        return ((chunks, H, 4 * LANES), BF16), ((chunks, 6, H, LANES), F32)

    def outs(nets, infos, chunks):
        return (shape((nets, 6, 8, LANES)), shape((infos, 8, LANES))) + tuple(
            shape(*k) for k in kept(chunks)
        )

    chunk = pltpu.VMEM((8, 8, LANES), F32)
    total = pltpu.VMEM((8, LANES), F32)
    spreads = (3, 6, H, LANES)
    params, *middle = call(
        middle_kernel, (shape(spreads),) + outs(3, 4, 4), (chunk, total), flops=10**9
    )(row, table)
    high = call(
        high_kernel,
        outs(6, 3, 1),
        (pltpu.VMEM(spreads, F32), chunk, total),
        flops=10**9,
    )(row, above, params)
    grad_w, grad_s, stat = call(
        last_kernel,
        (shape((H, H)), shape((8, H)), shape((first, 1, LANES))),
        (
            pltpu.VMEM((6, 6, 8, LANES), F32),
            *(pltpu.VMEM(*k) for k in kept(2)),
            pltpu.VMEM(spreads, F32),
            chunk,
            total,
            pltpu.VMEM((2, H, 4 * LANES), BF16),
            pltpu.VMEM((6, H, LANES), F32),
        ),
        limit=24 << 20,
        flops=10**9,
    )(row, below, above, mid_weight, params, *middle, *high)
    got = lax.all_to_all(stat, FIRST, 0, 0, tiled=True)
    part = call(sum_kernel, shape((second, 1, LANES)))(got)
    got = lax.all_to_all(part, SECOND, 0, 0, tiled=True)
    outs = call(
        lambda *refs: scale_kernel(count_x * count_y, *refs),
        (
            shape((1, 1, 2, H)),
            shape((1, 1, H)),
            shape((1, 1, H, H)),
            shape((1, 1, H)),
            shape((1, 1, H)),
            shape((1, 1)),
        ),
    )(got, grad_w, grad_s)
    return (*outs[:5], outs[5].reshape(()))


def solution(mesh):
    fine = Mesh(
        mesh.devices.reshape(8, 2, 2, 4, 4), ("z", "yh", "c", "yl", "x")
    )
    return jax.shard_map(
        local,
        mesh=fine,
        in_specs=(
            P(None, GX, GY, None),
            P(GX, GY, None),
            P(None, GX, GY, None),
            P(GX, GY, None),
            P(GX, GY, None),
            P(GX, GY, None, None),
            P(GX, GY, None),
            P(GX, GY, None, None),
            P(GX, GY, None),
            P(GX, GY, None),
        ),
        out_specs=(
            P(GX, GY, None, None),
            P(GX, GY, None),
            P(GX, GY, None, None),
            P(GX, GY, None),
            P(GX, GY, None),
            P(),
        ),
        check_vma=False,
    )
```

time: 91.9 us -> 78.1 us (0.85)
  Pallas kernels: 18.1 us -> 10.6 us
  waiting for transfers between devices: 14.1 us -> 10.4 us
  local copies, waits for them, and re-layouts: 2.33 us -> 0.01 us
    pallas_call x2 -> x4, Pallas kernels: 17.3 us -> 9.78 us  [the longest x1 4.92 us: local(): call(last_kernel, (shape((H, H)), shape((8, H)), shape((first, 1, LANES))...]
    unnamed x22 -> x2, local copies, waits for them, and re-layouts: 2.33 us -> 0.01 us
    ppermute x1, waiting for transfers between devices: 4.99 us -> 3.04 us  [local(): above = lax.ppermute(row, GY, [(j, i) for i, j in ring])]
    ppermute x1, waiting for transfers between devices: 6.03 us -> 4.27 us  [local(): below = lax.ppermute(row, GY, ring)]
  transfers between devices with their start and end apart: 4 -> 4, of which waited for: 4 -> 4; matrix products, arithmetic and copies ran while one was open for 0% -> 0% of each run, Pallas kernels for 0% -> 5%
where the time goes in v2:
time: 78.1 us; the launch traced here: 77.8 us
  blocking collectives  37.4 us (48%)
  starting transfers between devices  18.6 us (24%)
  Pallas kernels  10.6 us (14%)
  waiting for transfers between devices  10.4 us (13%)
    all_to_all x1, blocking collectives, local(): got = lax.all_to_all(stat, FIRST, 0, 0, tiled=True)  24.6 us
    all_to_all x1, blocking collectives, local(): got = lax.all_to_all(part, SECOND, 0, 0, tiled=True)  12.8 us
    ppermute x1, starting transfers between devices, local(): after = lax.ppermute(payload, GX, back)  8.79 us
    ppermute x1, starting transfers between devices, local(): above = lax.ppermute(row, GY, [(j, i) for i, j in ring])  5.96 us
    pallas_call x1, Pallas kernels, local(): call(last_kernel, (shape((H, H)), shape((8, H)), shape((first, 1, LANES))...  4.92 us
    ppermute x1, waiting for transfers between devices, local(): below = lax.ppermute(row, GY, ring)  4.27 us
    ppermute x1, waiting for transfers between devices, local(): above = lax.ppermute(row, GY, [(j, i) for i, j in ring])  3.04 us
    ppermute x1, waiting for transfers between devices, local(): before = lax.ppermute(payload, GX, forth)  2.1 us
  transfers between devices with their start and end apart: 4, of which 4 were waited for; matrix products, arithmetic and copies ran while one was open for 0% of the time, Pallas kernels for 5%

profile of v2, /device:TPU:1, one launch (start us, length us, event | category | flops | bytes accessed | tf_op | source)
XLA Modules:
  0.0 77.8 jit_solution(11574796869363990385)
XLA Ops:
  0.6 1.2 %shard_map.145 = (bf16[288,256]{1,0:T(8,128)(2,1)S(1)}, f32[8,384]{1,0:T(8,128)S(1)}) custom-call(f32[3,3,2,32]{3,2,1,0:T(2,128)} %bitcast.9, f32[3,3,32]{2,1,0:T(4,128)} %refs_1_.1, f32[3,3,2,32]{3,2,1,0:T(2,128)} %bitcast.10, f32[3,3,32]{2,1,0:T(4,128)} %refs_3_.1, f32[3,3,32]{2,1,0:T(4,128)} %refs_4_.1, bf16[1,1,2,256]{3,2,1,0:T(2,128)(2,1)} %refs_5_.1, ...), custom_call_target="tpu_custom_call" | custom-call | bytes 262144 | tf_op jit(solution)/shard_map/pallas_call | solution.py:517
  1.8 8.8 %collective-permute-start.1 = (bf16[288,256]{1,0:T(8,128)(2,1)S(1)}, bf16[288,256]{1,0:T(8,128)(2,1)S(1)}, u32[]{:S(2)}, u32[]{:S(2)}) collective-permute-start(bf16[288,256]{1,0:T(8,128)(2,1)S(1)} %get-tuple-element.26), channel_id=1, source_target_pairs={{16,0},{32,16},{48,32},{64,48},{80,64},{96,80},{112,96},{128,112},... | collective-permute-start | bytes 442376 | tf_op jit(solution)/shard_map/ppermute | solution.py:528
  10.6 2.0 %collective-permute-start = (bf16[288,256]{1,0:T(8,128)(2,1)S(1)}, bf16[288,256]{1,0:T(8,128)(2,1)S(1)}, u32[]{:S(2)}, u32[]{:S(2)}) collective-permute-start(bf16[288,256]{1,0:T(8,128)(2,1)S(1)} %get-tuple-element.26), channel_id=1, source_target_pairs={{0,16},{16,32},{32,48},{48,64},{64,80},{80,96},{96,112},{112,128},... | collective-permute-start | bytes 442376 | tf_op jit(solution)/shard_map/ppermute | solution.py:527
  12.6 1.0 %collective-permute-done.1 = bf16[288,256]{1,0:T(8,128)(2,1)S(1)} collective-permute-done((bf16[288,256]{1,0:T(8,128)(2,1)S(1)}, bf16[288,256]{1,0:T(8,128)(2,1)S(1)}, u32[]{:S(2)}, u32[]{:S(2)}) %collective-permute-start.1) | collective-permute-done | bytes 147488 | tf_op jit(solution)/shard_map/ppermute | solution.py:528
  13.6 2.1 %collective-permute-done = bf16[288,256]{1,0:T(8,128)(2,1)S(1)} collective-permute-done((bf16[288,256]{1,0:T(8,128)(2,1)S(1)}, bf16[288,256]{1,0:T(8,128)(2,1)S(1)}, u32[]{:S(2)}, u32[]{:S(2)}) %collective-permute-start) | collective-permute-done | bytes 147488 | tf_op jit(solution)/shard_map/ppermute | solution.py:527
  15.7 0.1 pad_maximum_fusion.mid_ref
  15.7 6.0 %collective-permute-start.3 = (bf16[3,288,256]{2,1,0:T(8,128)(2,1)S(1)}, bf16[3,288,256]{2,1,0:T(8,128)(2,1)S(1)}, u32[]{:S(2)}, u32[]{:S(2)}) collective-permute-start(bf16[3,288,256]{2,1,0:T(8,128)(2,1)S(1)} %pad_maximum_fusion.mid_ref), channel_id=1, source_target_pairs={{1,0},{2,1},{3,2},{4,3},{5,4},{6,5},{7,6},{8,7},{9,8},{10,9},{11,1... | collective-permute-start | bytes 1327112 | tf_op jit(solution)/shard_map/ppermute | solution.py:531
  21.7 1.9 %collective-permute-start.2 = (bf16[3,288,256]{2,1,0:T(8,128)(2,1)S(1)}, bf16[3,288,256]{2,1,0:T(8,128)(2,1)S(1)}, u32[]{:S(2)}, u32[]{:S(2)}) collective-permute-start(bf16[3,288,256]{2,1,0:T(8,128)(2,1)S(1)} %pad_maximum_fusion.mid_ref), channel_id=1, source_target_pairs={{0,1},{1,2},{2,3},{3,4},{4,5},{5,6},{6,7},{7,8},{8,9},{9,10},{10,1... | collective-permute-start | bytes 1327112 | tf_op jit(solution)/shard_map/ppermute | solution.py:532
  23.6 0.0 copy-start
  23.6 1.9 %shard_map.146 = (f32[3,6,256,128]{3,2,1,0:T(8,128)S(1)}, f32[3,6,8,128]{3,2,1,0:T(8,128)S(1)}, f32[4,8,128]{2,1,0:T(8,128)S(1)}, bf16[4,256,512]{2,1,0:T(8,128)(2,1)S(1)}, f32[4,6,256,128]{3,2,1,0:T(8,128)S(1)}) custom-call(bf16[3,288,256]{2,1,0:T(8,128)(2,1)S(1)} %pad_maximum_fusion.mid_ref, f32[8,384]{1,0:T(8,128)S(1)} %get-tuple-element.27.tab_ref), custom_call_target="tpu_custom_call" | custom-call | flops 1000000000 | bytes 262144 | tf_op jit(solution)/shard_map/pallas_call | solution.py:547
  25.6 3.0 %collective-permute-done.3.hi_ref = bf16[3,288,256]{2,1,0:T(8,128)(2,1)S(1)} collective-permute-done((bf16[3,288,256]{2,1,0:T(8,128)(2,1)S(1)}, bf16[3,288,256]{2,1,0:T(8,128)(2,1)S(1)}, u32[]{:S(2)}, u32[]{:S(2)}) %collective-permute-start.3) | collective-permute-done | bytes 442400 | tf_op jit(solution)/shard_map/ppermute | solution.py:531
  28.6 1.8 %shard_map.147 = (f32[6,6,8,128]{3,2,1,0:T(8,128)S(1)}, f32[3,8,128]{2,1,0:T(8,128)S(1)}, bf16[1,256,512]{2,1,0:T(8,128)(2,1)S(1)}, f32[1,6,256,128]{3,2,1,0:T(8,128)S(1)}) custom-call(bf16[3,288,256]{2,1,0:T(8,128)(2,1)S(1)} %pad_maximum_fusion.mid_ref, bf16[3,288,256]{2,1,0:T(8,128)(2,1)S(1)} %collective-permute-done.3.hi_ref, ...), custom_call_target="tpu_custom_call" | custom-call | flops 1000000000 | bytes 262144 | tf_op jit(solution)/shard_map/pallas_call | solution.py:550
  30.4 4.3 %collective-permute-done.2.lo_ref = bf16[3,288,256]{2,1,0:T(8,128)(2,1)S(1)} collective-permute-done((bf16[3,288,256]{2,1,0:T(8,128)(2,1)S(1)}, bf16[3,288,256]{2,1,0:T(8,128)(2,1)S(1)}, u32[]{:S(2)}, u32[]{:S(2)}) %collective-permute-start.2) | collective-permute-done | bytes 442400 | tf_op jit(solution)/shard_map/ppermute | solution.py:532
  34.6 0.0 copy-done
  34.6 4.9 %shard_map.148 = (f32[256,256]{1,0:T(8,128)S(1)}, f32[8,256]{1,0:T(8,128)S(1)}, f32[16,1,128]{2,1,0:T(1,128)S(1)}) custom-call(bf16[3,288,256]{2,1,0:T(8,128)(2,1)S(1)} %pad_maximum_fusion.mid_ref, bf16[3,288,256]{2,1,0:T(8,128)(2,1)S(1)} %collective-permute-done.2.lo_ref, bf16[3,288,256]{2,1,0:T(8,128)(2,1)S(1)} %collective-permute-done.3.hi_ref, ...), custom_call_target="tpu_custom_call" | custom-call | flops 1000000000 | bytes 262144 | tf_op jit(solution)/shard_map/pallas_call | solution.py:556
  39.6 24.6 %all_to_all.10.got_ref = f32[16,1,128]{2,1,0:T(1,128)S(1)} all-to-all(f32[16,1,128]{2,1,0:T(1,128)S(1)} %get-tuple-element.37), channel_id=1, replica_groups=mesh['z'=8,'yh'=2,'c'=2,'yl'=4,'x'=4] {'z','c'}, dimensions={0} | all-to-all | bytes 16384 | tf_op jit(solution)/shard_map/all_to_all | solution.py:571
  64.2 12.8 %all_to_all.11.refs_0_ = f32[32,1,128]{2,1,0:T(1,128)S(1)} all-to-all(f32[32,1,128]{2,1,0:T(1,128)S(1)} %shard_map.149), channel_id=1, replica_groups=mesh['z'=8,'yh'=2,'c'=2,'yl'=4,'x'=4] {'yh','yl','x'}, dimensions={0} | all-to-all | bytes 32768 | tf_op jit(solution)/shard_map/all_to_all | solution.py:573
  77.0 0.8 %shard_map.150 = (f32[1,1,2,256]{3,2,1,0:T(2,128)}, f32[1,1,256]{2,1,0:T(1,128)}, f32[1,1,256,256]{3,2,1,0:T(8,128)}, f32[1,1,256]{2,1,0:T(1,128)}, f32[1,1,256]{2,1,0:T(1,128)}, /*index=5*/f32[1,1]{1,0:T(1,128)}) custom-call(f32[32,1,128]{2,1,0:T(1,128)S(1)} %all_to_all.11.refs_0_, f32[256,256]{1,0:T(8,128)S(1)} %get-tuple-element.38.refs_1_, ...), custom_call_target="tpu_custom_call" | custom-call | bytes 262144 | tf_op jit(solution)/shard_map/pallas_call | solution.py:574
  (1 shorter events, 0.0 us)
Async XLA Ops:
  1.8 11.8 %collective-permute-start.1 = (bf16[288,256]{1,0:T(8,128)(2,1)S(1)}, bf16[288,256]{1,0:T(8,128)(2,1)S(1)}, u32[]{:S(2)}, u32[]{:S(2)}) collective-permute-start(bf16[288,256]{1,0:T(8,128)(2,1)S(1)} %get-tuple-element.26), channel_id=1, source_target_pairs={{16,0},{32,16},{48,32},{64,48},{80,64},{96,80},{112,96},{128,112},... | collective-permute-start | bytes 442376 | tf_op jit(solution)/shard_map/ppermute | solution.py:528
  10.6 5.1 %collective-permute-start = (bf16[288,256]{1,0:T(8,128)(2,1)S(1)}, bf16[288,256]{1,0:T(8,128)(2,1)S(1)}, u32[]{:S(2)}, u32[]{:S(2)}) collective-permute-start(bf16[288,256]{1,0:T(8,128)(2,1)S(1)} %get-tuple-element.26), channel_id=1, source_target_pairs={{0,16},{16,32},{32,48},{48,64},{64,80},{80,96},{96,112},{112,128},... | collective-permute-start | bytes 442376 | tf_op jit(solution)/shard_map/ppermute | solution.py:527
  15.7 12.9 %collective-permute-start.3 = (bf16[3,288,256]{2,1,0:T(8,128)(2,1)S(1)}, bf16[3,288,256]{2,1,0:T(8,128)(2,1)S(1)}, u32[]{:S(2)}, u32[]{:S(2)}) collective-permute-start(bf16[3,288,256]{2,1,0:T(8,128)(2,1)S(1)} %pad_maximum_fusion.mid_ref), channel_id=1, source_target_pairs={{1,0},{2,1},{3,2},{4,3},{5,4},{6,5},{7,6},{8,7},{9,8},{10,9},{11,1... | collective-permute-start | bytes 1327112 | tf_op jit(solution)/shard_map/ppermute | solution.py:531
  21.7 13.0 %collective-permute-start.2 = (bf16[3,288,256]{2,1,0:T(8,128)(2,1)S(1)}, bf16[3,288,256]{2,1,0:T(8,128)(2,1)S(1)}, u32[]{:S(2)}, u32[]{:S(2)}) collective-permute-start(bf16[3,288,256]{2,1,0:T(8,128)(2,1)S(1)} %pad_maximum_fusion.mid_ref), channel_id=1, source_target_pairs={{0,1},{1,2},{2,3},{3,4},{4,5},{5,6},{6,7},{7,8},{8,9},{9,10},{10,1... | collective-permute-start | bytes 1327112 | tf_op jit(solution)/shard_map/ppermute | solution.py:532
  23.6 11.0 %copy-start = (bf16[1,1,256,256]{3,2,1,0:T(8,128)(2,1)S(1)}, bf16[1,1,256,256]{3,2,1,0:T(8,128)(2,1)}, u32[]{:S(2)}) copy-start(bf16[1,1,256,256]{3,2,1,0:T(8,128)(2,1)} %w_ref.1) | copy-start | bytes 393220

commit v3 on v2

--- a/solution.py
+++ b/solution.py
@@ -1,3 +1,5 @@
+import functools
+
 import jax
 import jax.numpy as jnp
 from jax import lax
@@ -96,9 +98,13 @@
                 src[a, b : b + 1, :],
                 ones,
             ]
-            pieces[PLACE[a, b]] = jnp.concatenate(rows, axis=0)
+            pieces[a, b] = jnp.concatenate(rows, axis=0)
     blank = jnp.concatenate([zeros] * 8, axis=0)
-    order = [pieces.get(32 * k, blank) for k in range(12)]
+    turn = lax.rem(lax.axis_index("x"), 2) == 1
+    placed = {
+        at: jnp.where(turn, pieces[a, 2 - b], pieces[a, b]) for (a, b), at in PLACE.items()
+    }
+    order = [placed.get(32 * k, blank) for k in range(12)]
     tabs = [jnp.concatenate(order[4 * k : 4 * k + 4], axis=1) for k in range(3)]
     for k in range(3):
         tab_ref[:, 128 * k : 128 * k + 128] = tabs[k]
@@ -114,7 +120,8 @@
             b_mid[0].astype(F32),
             w_out[0].astype(F32),
             jnp.ones((1, H), F32),
-            jnp.zeros((2, H), F32),
+            jnp.where(turn, -1.0, 1.0) * jnp.ones((1, H), F32),
+            jnp.zeros((1, H), F32),
         ],
         axis=0,
     )
@@ -139,7 +146,7 @@
         for big_a, big_b in regions:
             p = 0 if big_a == 0 else 2 if big_a == 4 else 1
             q = 0 if big_b == 0 else 2 if big_b == 4 else 1
-            at = PLACE[(2, big_a - 1, 0)[p], (2, big_b - 1, 0)[q]]
+            at = PLACE[(2, big_a - 1, 0)[p], (0, big_b - 1, 2)[q]]
             parts.append(points[q][p][:, at : at + SPAN])
         parts += [blank] * (4 - len(parts))
         chunk_ref[c] = jnp.concatenate(parts, axis=1)
@@ -169,10 +176,11 @@
     return off_x, off_y, wide_x * wide_y / SPAN * flag, own
 
 
-def put_coefs(coef_ref, rows, off_x, off_y, nets):
+def put_coefs(coef_ref, rows, off_x, off_y, nets, small):
     pos_x, pos_y, diff, vel_x, vel_y, rate = rows[:6]
+    way = small[30:31, 0:LANES]
     coords_x = {p: pos_x + (off_x - float(p)) for p, _, _ in nets}
-    coords_y = {q: pos_y + (off_y - float(q)) for _, q, _ in nets}
+    coords_y = {q: pos_y + way * (off_y - float(q)) for _, q, _ in nets}
     bumps_x = {p: bump(t) for p, t in coords_x.items()}
     bumps_y = {q: bump(s) for q, s in coords_y.items()}
     for n, (p, q, present) in enumerate(nets):
@@ -275,7 +283,7 @@
     rows = gather_rows(chunk_ref, MIDDLE, [None, points, None])
     off_x, off_y, area, own = frame(MIDDLE, rows[7])
     nets = [(p - 1, 0, smalls[p][29:30, 0:LANES]) for p in range(3)]
-    put_coefs(coef_ref, rows, off_x, off_y, nets)
+    put_coefs(coef_ref, rows, off_x, off_y, nets, smalls[1])
     spread(smalls, par_ref)
     total_ref[...] = jnp.zeros((8, LANES), F32)
     for c in range(4):
@@ -302,7 +310,7 @@
     off_x, off_y, area, _ = frame(layout, rows[7])
     nets = [(p - 1, 0, smalls[p][29:30, 0:LANES]) for p in range(3)]
     nets += [(p - 1, q, far[p][29:30, 0:LANES]) for p in range(3)]
-    put_coefs(coef_ref, rows, off_x, off_y, nets)
+    put_coefs(coef_ref, rows, off_x, off_y, nets, smalls[1])
     spread(far, side_par)
     total_ref[...] = jnp.zeros((8, LANES), F32)
     for k, c in enumerate(range(3, len(layout))):
@@ -389,41 +397,67 @@
     own = jnp.where(line < 4, info_m[3], 0.0)
     loss = jnp.sum(own * area * residual * residual)
     total_ref[...] = 2.0 * area * residual
-    acc_ref[...] = jnp.zeros(acc_ref.shape, F32)
-    gw_ref[...] = jnp.zeros((H, H), F32)
     w1, w2, pw = par_ref.at[1, 0], par_ref.at[1, 1], par_ref.at[1, 5]
     places = [(coef_m, c, s_m, state_m, c) for c in range(4)]
     places += [(coef_h, 3, s_h, state_h, 0), (coef_l, 3, s_l, state_l, 0)]
     places += [(coef_l, 4, s_l, state_l, 1)]
-    for row, (coef_ref, c, s_ref, state_ref, k) in enumerate(places):
-        xi, eta, _, _, _, c3 = coefs(coef_ref, 1, c)
-        adjoint = total_ref[row : row + 1, :]
-        h1 = state_ref[k, 0]
-        scale = state_ref[k, 2] * adjoint
-        d_base = scale * state_ref[k, 3]
-        acc_ref[5] += state_ref[k, 1] * adjoint
-        acc_ref[4] += d_base
-        d_ref[row % 2, :, 0:LANES] = d_base.astype(BF16)
-        d_ref[row % 2, :, LANES : 2 * LANES] = (scale * state_ref[k, 4]).astype(BF16)
-        d_ref[row % 2, :, 2 * LANES : 3 * LANES] = (scale * state_ref[k, 5]).astype(BF16)
-        d_ref[row % 2, :, 3 * LANES :] = (scale * c3).astype(BF16)
-        d_mixed = d_ref[row % 2]
-        d_streams = jnp.dot(w_ref[0, 0], d_mixed, preferred_element_type=F32)
-        gw_ref[...] += lax.dot_general(
-            s_ref[k], d_mixed, (((1,), (1,)), ((), ())), preferred_element_type=F32
-        )
-        ds0 = d_streams[:, 0:LANES]
-        ds1 = d_streams[:, LANES : 2 * LANES]
-        ds2 = d_streams[:, 2 * LANES : 3 * LANES]
-        ds3 = d_streams[:, 3 * LANES :]
-        d1 = 1.0 - h1 * h1
-        cross = w1[...] * ds1 + w2[...] * ds2
-        d_pre = d1 * (ds0 + pw[...] * ds3 * (3.0 * d1 - 2.0) - (4.0 * h1) * cross)
-        d1x2 = 2.0 * d1
-        acc_ref[0] += d1x2 * ds1 + xi * d_pre
-        acc_ref[1] += d1x2 * ds2 + eta * d_pre
-        acc_ref[2] += d_pre
-        acc_ref[3] += h1 * d1 * ds3
+
+    def put(ref, parts, first):
+        value = functools.reduce(lambda one, two: one + two, parts)
+        ref[...] = value if first else ref[...] + value
+
+    def cotangents(group, first):
+        base, mix = [], []
+        for row in group:
+            coef_ref, c, _, state_ref, k = places[row]
+            c3 = coef_ref[1, 5, c : c + 1, :]
+            adjoint = total_ref[row : row + 1, :]
+            scale = state_ref[k, 2] * adjoint
+            d_base = scale * state_ref[k, 3]
+            base.append(d_base)
+            mix.append(state_ref[k, 1] * adjoint)
+            d_ref[row, :, 0:LANES] = d_base.astype(BF16)
+            d_ref[row, :, LANES : 2 * LANES] = (scale * state_ref[k, 4]).astype(BF16)
+            d_ref[row, :, 2 * LANES : 3 * LANES] = (scale * state_ref[k, 5]).astype(BF16)
+            d_ref[row, :, 3 * LANES :] = (scale * c3).astype(BF16)
+        put(acc_ref.at[4], base, first)
+        put(acc_ref.at[5], mix, first)
+
+    groups = ((0, 1), (2, 3), (4, 5), (6,))
+    cotangents(groups[0], True)
+    for g, group in enumerate(groups):
+        d_streams = [
+            jnp.dot(w_ref[0, 0], d_ref[row], preferred_element_type=F32) for row in group
+        ]
+        terms = [
+            lax.dot_general(
+                places[row][2][places[row][4]],
+                d_ref[row],
+                (((1,), (1,)), ((), ())),
+                preferred_element_type=F32,
+            )
+            for row in group
+        ]
+        if g + 1 < len(groups):
+            cotangents(groups[g + 1], False)
+        put(gw_ref, terms, g == 0)
+        parts = [[], [], [], []]
+        for row, ds in zip(group, d_streams):
+            coef_ref, c, _, state_ref, k = places[row]
+            xi, eta = coef_ref[1, 0, c : c + 1, :], coef_ref[1, 1, c : c + 1, :]
+            h1 = state_ref[k, 0]
+            ds0, ds1 = ds[:, 0:LANES], ds[:, LANES : 2 * LANES]
+            ds2, ds3 = ds[:, 2 * LANES : 3 * LANES], ds[:, 3 * LANES :]
+            d1 = 1.0 - h1 * h1
+            cross = w1[...] * ds1 + w2[...] * ds2
+            d_pre = d1 * (ds0 + pw[...] * ds3 * (3.0 * d1 - 2.0) - (4.0 * h1) * cross)
+            d1x2 = 2.0 * d1
+            parts[0].append(d1x2 * ds1 + xi * d_pre)
+            parts[1].append(d1x2 * ds2 + eta * d_pre)
+            parts[2].append(d_pre)
+            parts[3].append(h1 * d1 * ds3)
+        for k, part in enumerate(parts):
+            put(acc_ref.at[k], part, g == 0)
     sums = [jnp.sum(acc_ref[k], axis=1, keepdims=True) for k in range(6)]
     turn = -16.0 * sums[3]
     grid = jnp.concatenate(
@@ -523,13 +557,13 @@
         limit=16 << 20,
     )(*(pltpu.with_memory_space_constraint(x, pltpu.HBM) for x in inputs))
     forth = [(i, i + 1) for i in range(count_x - 1)]
-    back = [(i + 1, i) for i in range(count_x - 1)]
+    after = lax.ppermute(payload, GX, [(j, i) for i, j in forth])
     before = lax.ppermute(payload, GX, forth)
-    after = lax.ppermute(payload, GX, back)
     row = jnp.stack([before, payload, after])
-    ring = [(i, (i + 1) % count_y) for i in range(count_y)]
-    above = lax.ppermute(row, GY, [(j, i) for i, j in ring])
-    below = lax.ppermute(row, GY, ring)
+    pairs = [(i, i ^ 1) for i in range(count_y)]
+    bonds = [(i, (i + 1) % count_y) for i in range(1, count_y, 2)]
+    above = lax.ppermute(row, GY, pairs)
+    below = lax.ppermute(row, GY, bonds + [(j, i) for i, j in bonds])
     first = lax.axis_size(FIRST)
     second = lax.axis_size(SECOND)
 
@@ -562,7 +596,7 @@
             pltpu.VMEM(spreads, F32),
             chunk,
             total,
-            pltpu.VMEM((2, H, 4 * LANES), BF16),
+            pltpu.VMEM((7, H, 4 * LANES), BF16),
             pltpu.VMEM((6, H, LANES), F32),
         ),
         limit=24 << 20,

time: 78.1 us -> 75.9 us (0.972)
  blocking collectives: 37.4 us -> 35.5 us
    all_to_all x1, blocking collectives: 24.6 us -> 22.5 us  [local(): got = lax.all_to_all(stat, FIRST, 0, 0, tiled=True)]
where the time goes in v3:
time: 75.9 us; the launch traced here: 75.6 us
  blocking collectives  35.5 us (47%)
  starting transfers between devices  19.2 us (25%)
  Pallas kernels  10.5 us (14%)
  waiting for transfers between devices  9.66 us (13%)
    all_to_all x1, blocking collectives, local(): got = lax.all_to_all(stat, FIRST, 0, 0, tiled=True)  22.5 us
    all_to_all x1, blocking collectives, local(): got = lax.all_to_all(part, SECOND, 0, 0, tiled=True)  12.9 us
    ppermute x1, starting transfers between devices, local(): after = lax.ppermute(payload, GX, [(j, i) for i, j in forth])  8.79 us
    ppermute x1, starting transfers between devices, local(): below = lax.ppermute(row, GY, bonds + [(j, i) for i, j in bonds])  5.29 us
    pallas_call x1, Pallas kernels, local(): call(last_kernel, (shape((H, H)), shape((8, H)), shape((first, 1, LANES))...  4.8 us
    ppermute x1, waiting for transfers between devices, local(): below = lax.ppermute(row, GY, bonds + [(j, i) for i, j in bonds])  4.08 us
    ppermute x1, starting transfers between devices, local(): above = lax.ppermute(row, GY, pairs)  3.12 us
    ppermute x1, waiting for transfers between devices, local(): above = lax.ppermute(row, GY, pairs)  2.5 us
  transfers between devices with their start and end apart: 4, of which 4 were waited for; matrix products, arithmetic and copies ran while one was open for 0% of the time, Pallas kernels for 5%

profile of v3, /device:TPU:1, one launch (start us, length us, event | category | flops | bytes accessed | tf_op | source)
XLA Modules:
  0.0 75.6 jit_solution(3092325171931441460)
XLA Ops:
  0.6 1.2 %shard_map.145 = (bf16[288,256]{1,0:T(8,128)(2,1)S(1)}, f32[8,384]{1,0:T(8,128)S(1)}) custom-call(f32[3,3,2,32]{3,2,1,0:T(2,128)} %bitcast.9, f32[3,3,32]{2,1,0:T(4,128)} %refs_1_.1, f32[3,3,2,32]{3,2,1,0:T(2,128)} %bitcast.10, f32[3,3,32]{2,1,0:T(4,128)} %refs_3_.1, f32[3,3,32]{2,1,0:T(4,128)} %refs_4_.1, bf16[1,1,2,256]{3,2,1,0:T(2,128)(2,1)} %refs_5_.1, ...), custom_call_target="tpu_custom_call" | custom-call | bytes 262144 | tf_op jit(solution)/shard_map/pallas_call | solution.py:551
  1.8 8.8 %collective-permute-start.1 = (bf16[288,256]{1,0:T(8,128)(2,1)S(1)}, bf16[288,256]{1,0:T(8,128)(2,1)S(1)}, u32[]{:S(2)}, u32[]{:S(2)}) collective-permute-start(bf16[288,256]{1,0:T(8,128)(2,1)S(1)} %get-tuple-element.26), channel_id=1, source_target_pairs={{16,0},{32,16},{48,32},{64,48},{80,64},{96,80},{112,96},{128,112},... | collective-permute-start | bytes 442376 | tf_op jit(solution)/shard_map/ppermute | solution.py:560
  10.6 2.0 %collective-permute-start = (bf16[288,256]{1,0:T(8,128)(2,1)S(1)}, bf16[288,256]{1,0:T(8,128)(2,1)S(1)}, u32[]{:S(2)}, u32[]{:S(2)}) collective-permute-start(bf16[288,256]{1,0:T(8,128)(2,1)S(1)} %get-tuple-element.26), channel_id=1, source_target_pairs={{0,16},{16,32},{32,48},{48,64},{64,80},{80,96},{96,112},{112,128},... | collective-permute-start | bytes 442376 | tf_op jit(solution)/shard_map/ppermute | solution.py:561
  12.6 1.0 %collective-permute-done.1 = bf16[288,256]{1,0:T(8,128)(2,1)S(1)} collective-permute-done((bf16[288,256]{1,0:T(8,128)(2,1)S(1)}, bf16[288,256]{1,0:T(8,128)(2,1)S(1)}, u32[]{:S(2)}, u32[]{:S(2)}) %collective-permute-start.1) | collective-permute-done | bytes 147488 | tf_op jit(solution)/shard_map/ppermute | solution.py:560
  13.6 2.1 %collective-permute-done = bf16[288,256]{1,0:T(8,128)(2,1)S(1)} collective-permute-done((bf16[288,256]{1,0:T(8,128)(2,1)S(1)}, bf16[288,256]{1,0:T(8,128)(2,1)S(1)}, u32[]{:S(2)}, u32[]{:S(2)}) %collective-permute-start) | collective-permute-done | bytes 147488 | tf_op jit(solution)/shard_map/ppermute | solution.py:561
  15.7 0.1 pad_maximum_fusion.mid_ref
  15.7 3.1 %collective-permute-start.3 = (bf16[3,288,256]{2,1,0:T(8,128)(2,1)S(1)}, bf16[3,288,256]{2,1,0:T(8,128)(2,1)S(1)}, u32[]{:S(2)}, u32[]{:S(2)}) collective-permute-start(bf16[3,288,256]{2,1,0:T(8,128)(2,1)S(1)} %pad_maximum_fusion.mid_ref), channel_id=1, source_target_pairs={{0,1},{1,0},{2,3},{3,2},{4,5},{5,4},{6,7},{7,6},{8,9},{9,8},{10,11... | collective-permute-start | bytes 1327112 | tf_op jit(solution)/shard_map/ppermute | solution.py:565
  18.8 5.3 %collective-permute-start.2 = (bf16[3,288,256]{2,1,0:T(8,128)(2,1)S(1)}, bf16[3,288,256]{2,1,0:T(8,128)(2,1)S(1)}, u32[]{:S(2)}, u32[]{:S(2)}) collective-permute-start(bf16[3,288,256]{2,1,0:T(8,128)(2,1)S(1)} %pad_maximum_fusion.mid_ref), channel_id=1, source_target_pairs={{1,2},{3,4},{5,6},{7,8},{9,10},{11,12},{13,14},{15,0},{2,1},{4,3},... | collective-permute-start | bytes 1327112 | tf_op jit(solution)/shard_map/ppermute | solution.py:566
  24.1 0.0 copy-start
  24.2 1.9 %shard_map.146 = (f32[3,6,256,128]{3,2,1,0:T(8,128)S(1)}, f32[3,6,8,128]{3,2,1,0:T(8,128)S(1)}, f32[4,8,128]{2,1,0:T(8,128)S(1)}, bf16[4,256,512]{2,1,0:T(8,128)(2,1)S(1)}, f32[4,6,256,128]{3,2,1,0:T(8,128)S(1)}) custom-call(bf16[3,288,256]{2,1,0:T(8,128)(2,1)S(1)} %pad_maximum_fusion.mid_ref, f32[8,384]{1,0:T(8,128)S(1)} %get-tuple-element.27.tab_ref), custom_call_target="tpu_custom_call" | custom-call | flops 1000000000 | bytes 262144 | tf_op jit(solution)/shard_map/pallas_call | solution.py:581
  26.1 2.5 %collective-permute-done.3.hi_ref = bf16[3,288,256]{2,1,0:T(8,128)(2,1)S(1)} collective-permute-done((bf16[3,288,256]{2,1,0:T(8,128)(2,1)S(1)}, bf16[3,288,256]{2,1,0:T(8,128)(2,1)S(1)}, u32[]{:S(2)}, u32[]{:S(2)}) %collective-permute-start.3) | collective-permute-done | bytes 442400 | tf_op jit(solution)/shard_map/ppermute | solution.py:565
  28.6 1.8 %shard_map.147 = (f32[6,6,8,128]{3,2,1,0:T(8,128)S(1)}, f32[3,8,128]{2,1,0:T(8,128)S(1)}, bf16[1,256,512]{2,1,0:T(8,128)(2,1)S(1)}, f32[1,6,256,128]{3,2,1,0:T(8,128)S(1)}) custom-call(bf16[3,288,256]{2,1,0:T(8,128)(2,1)S(1)} %pad_maximum_fusion.mid_ref, bf16[3,288,256]{2,1,0:T(8,128)(2,1)S(1)} %collective-permute-done.3.hi_ref, ...), custom_call_target="tpu_custom_call" | custom-call | flops 1000000000 | bytes 262144 | tf_op jit(solution)/shard_map/pallas_call | solution.py:584
  30.4 4.1 %collective-permute-done.2.lo_ref = bf16[3,288,256]{2,1,0:T(8,128)(2,1)S(1)} collective-permute-done((bf16[3,288,256]{2,1,0:T(8,128)(2,1)S(1)}, bf16[3,288,256]{2,1,0:T(8,128)(2,1)S(1)}, u32[]{:S(2)}, u32[]{:S(2)}) %collective-permute-start.2) | collective-permute-done | bytes 442400 | tf_op jit(solution)/shard_map/ppermute | solution.py:566
  34.4 0.0 copy-done
  34.4 4.8 %shard_map.148 = (f32[256,256]{1,0:T(8,128)S(1)}, f32[8,256]{1,0:T(8,128)S(1)}, f32[16,1,128]{2,1,0:T(1,128)S(1)}) custom-call(bf16[3,288,256]{2,1,0:T(8,128)(2,1)S(1)} %pad_maximum_fusion.mid_ref, bf16[3,288,256]{2,1,0:T(8,128)(2,1)S(1)} %collective-permute-done.2.lo_ref, bf16[3,288,256]{2,1,0:T(8,128)(2,1)S(1)} %collective-permute-done.3.hi_ref, ...), custom_call_target="tpu_custom_call" | custom-call | flops 1000000000 | bytes 262144 | tf_op jit(solution)/shard_map/pallas_call | solution.py:590
  39.2 22.5 %all_to_all.10.got_ref = f32[16,1,128]{2,1,0:T(1,128)S(1)} all-to-all(f32[16,1,128]{2,1,0:T(1,128)S(1)} %get-tuple-element.37), channel_id=1, replica_groups=mesh['z'=8,'yh'=2,'c'=2,'yl'=4,'x'=4] {'z','c'}, dimensions={0} | all-to-all | bytes 16384 | tf_op jit(solution)/shard_map/all_to_all | solution.py:605
  61.8 12.9 %all_to_all.11.refs_0_ = f32[32,1,128]{2,1,0:T(1,128)S(1)} all-to-all(f32[32,1,128]{2,1,0:T(1,128)S(1)} %shard_map.149), channel_id=1, replica_groups=mesh['z'=8,'yh'=2,'c'=2,'yl'=4,'x'=4] {'yh','yl','x'}, dimensions={0} | all-to-all | bytes 32768 | tf_op jit(solution)/shard_map/all_to_all | solution.py:607
  74.7 0.8 %shard_map.150 = (f32[1,1,2,256]{3,2,1,0:T(2,128)}, f32[1,1,256]{2,1,0:T(1,128)}, f32[1,1,256,256]{3,2,1,0:T(8,128)}, f32[1,1,256]{2,1,0:T(1,128)}, f32[1,1,256]{2,1,0:T(1,128)}, /*index=5*/f32[1,1]{1,0:T(1,128)}) custom-call(f32[32,1,128]{2,1,0:T(1,128)S(1)} %all_to_all.11.refs_0_, f32[256,256]{1,0:T(8,128)S(1)} %get-tuple-element.38.refs_1_, ...), custom_call_target="tpu_custom_call" | custom-call | bytes 262144 | tf_op jit(solution)/shard_map/pallas_call | solution.py:608
  (1 shorter events, 0.0 us)
Async XLA Ops:
  1.8 11.8 %collective-permute-start.1 = (bf16[288,256]{1,0:T(8,128)(2,1)S(1)}, bf16[288,256]{1,0:T(8,128)(2,1)S(1)}, u32[]{:S(2)}, u32[]{:S(2)}) collective-permute-start(bf16[288,256]{1,0:T(8,128)(2,1)S(1)} %get-tuple-element.26), channel_id=1, source_target_pairs={{16,0},{32,16},{48,32},{64,48},{80,64},{96,80},{112,96},{128,112},... | collective-permute-start | bytes 442376 | tf_op jit(solution)/shard_map/ppermute | solution.py:560
  10.6 5.1 %collective-permute-start = (bf16[288,256]{1,0:T(8,128)(2,1)S(1)}, bf16[288,256]{1,0:T(8,128)(2,1)S(1)}, u32[]{:S(2)}, u32[]{:S(2)}) collective-permute-start(bf16[288,256]{1,0:T(8,128)(2,1)S(1)} %get-tuple-element.26), channel_id=1, source_target_pairs={{0,16},{16,32},{32,48},{48,64},{64,80},{80,96},{96,112},{112,128},... | collective-permute-start | bytes 442376 | tf_op jit(solution)/shard_map/ppermute | solution.py:561
  15.7 12.9 %collective-permute-start.3 = (bf16[3,288,256]{2,1,0:T(8,128)(2,1)S(1)}, bf16[3,288,256]{2,1,0:T(8,128)(2,1)S(1)}, u32[]{:S(2)}, u32[]{:S(2)}) collective-permute-start(bf16[3,288,256]{2,1,0:T(8,128)(2,1)S(1)} %pad_maximum_fusion.mid_ref), channel_id=1, source_target_pairs={{0,1},{1,0},{2,3},{3,2},{4,5},{5,4},{6,7},{7,6},{8,9},{9,8},{10,11... | collective-permute-start | bytes 1327112 | tf_op jit(solution)/shard_map/ppermute | solution.py:565
  18.8 15.6 %collective-permute-start.2 = (bf16[3,288,256]{2,1,0:T(8,128)(2,1)S(1)}, bf16[3,288,256]{2,1,0:T(8,128)(2,1)S(1)}, u32[]{:S(2)}, u32[]{:S(2)}) collective-permute-start(bf16[3,288,256]{2,1,0:T(8,128)(2,1)S(1)} %pad_maximum_fusion.mid_ref), channel_id=1, source_target_pairs={{1,2},{3,4},{5,6},{7,8},{9,10},{11,12},{13,14},{15,0},{2,1},{4,3},... | collective-permute-start | bytes 1327112 | tf_op jit(solution)/shard_map/ppermute | solution.py:566
  24.1 10.3 %copy-start = (bf16[1,1,256,256]{3,2,1,0:T(8,128)(2,1)S(1)}, bf16[1,1,256,256]{3,2,1,0:T(8,128)(2,1)}, u32[]{:S(2)}) copy-start(bf16[1,1,256,256]{3,2,1,0:T(8,128)(2,1)} %w_ref.1) | copy-start | bytes 393220

commit v4 on v3

--- a/solution.py
+++ b/solution.py
@@ -17,25 +17,26 @@
 BF16 = jnp.bfloat16
 
 MIDDLE = (
-    ((0, 1), (1, 1), (0, 3), (1, 3)),
-    ((3, 1), (4, 1), (3, 3), (4, 3)),
     ((0, 2), (1, 2), (3, 2), (4, 2)),
-    ((2, 1), (2, 2), (2, 3)),
+    ((0, 3), (1, 3), (3, 3), (4, 3)),
+    ((0, 1), (1, 1), (3, 1), (4, 1)),
 )
 HIGH = (
     ((0, 3), (0, 4), (1, 3), (1, 4)),
     ((3, 3), (3, 4), (4, 3), (4, 4)),
     ((2, 3), (2, 4)),
     ((0, 4), (1, 4), (3, 4), (4, 4)),
+    ((2, 2), (2, 3), (2, 4)),
 )
 BELOW = (
     ((0, 0), (0, 1), (1, 0), (1, 1)),
     ((3, 0), (3, 1), (4, 0), (4, 1)),
     ((2, 0), (2, 1)),
     ((0, 0), (1, 0), (3, 0), (4, 0)),
-    ((2, 0), (2, 4)),
+    ((2, 0), (2, 1)),
 )
-WINDOW = MIDDLE + (HIGH[3], BELOW[3], BELOW[4])
+EARLY = (MIDDLE[0], MIDDLE[1], HIGH[3], HIGH[4])
+LATE = (MIDDLE[2], BELOW[3], BELOW[4])
 PLACE = {
     (0, 0): 0,
     (0, 1): 32,
@@ -132,7 +133,7 @@
 
 
 def small_rows(ref):
-    return [ref[p, H:ROWS, :].astype(F32) for p in range(3)]
+    return [ref[2 - p, H:ROWS, :].astype(F32) for p in range(3)]
 
 
 def tables(smalls):
@@ -197,6 +198,9 @@
         coef_ref[n, 3] = -2.0 * diff * window_x + vel_x * window
         coef_ref[n, 4] = -2.0 * diff * window_y + vel_y * window
         coef_ref[n, 5] = -diff * window
+    left = lax.broadcasted_iota(jnp.int32, (8, LANES), 1) < LANES // 2
+    for k in range(6):
+        coef_ref[len(nets), k] = jnp.where(left, coef_ref[0, k], coef_ref[2, k])
 
 
 def spread(smalls, par_ref):
@@ -230,7 +234,11 @@
         ],
         axis=1,
     )
-    mixed = jnp.dot(weights, streams, preferred_element_type=F32)
+    mixed = [jnp.dot(w, streams, preferred_element_type=F32) for w in weights]
+    if len(mixed) == 2:
+        lane = lax.broadcasted_iota(jnp.int32, (1, 4 * LANES), 1)
+        mixed = [jnp.where(lane % LANES < LANES // 2, *mixed)]
+    mixed = mixed[0]
     h2 = jnp.tanh(mixed[:, 0:LANES] + par_ref[n, 3])
     gx = mixed[:, LANES : 2 * LANES]
     gy = mixed[:, 2 * LANES : 3 * LANES]
@@ -285,62 +293,54 @@
     nets = [(p - 1, 0, smalls[p][29:30, 0:LANES]) for p in range(3)]
     put_coefs(coef_ref, rows, off_x, off_y, nets, smalls[1])
     spread(smalls, par_ref)
+    left = lax.broadcasted_iota(jnp.int32, (H, LANES), 1) < LANES // 2
+    for k in range(6):
+        par_ref[3, k] = jnp.where(left, par_ref[0, k], par_ref[2, k])
     total_ref[...] = jnp.zeros((8, LANES), F32)
-    for c in range(4):
-        own_step(
-            total_ref, coef_ref, 1, c, par_ref, mid_ref[1, 0:H, :], c, s_ref, state_ref
-        )
-    for p, c in ((0, 0), (2, 1), (0, 2), (2, 2)):
-        near_step(total_ref, coef_ref, p, c, par_ref, p, mid_ref[p, 0:H, :])
+    weights = [mid_ref[2 - p, 0:H, :] for p in range(3)]
+    for c in range(3):
+        own_step(total_ref, coef_ref, 1, c, par_ref, weights[1:2], c, s_ref, state_ref)
+    for c in range(3):
+        near_step(total_ref, coef_ref, 3, c, par_ref, 3, weights[0::2])
     info_ref[0] = total_ref[...]
     info_ref[1] = area
     info_ref[2] = rows[6]
     info_ref[3] = own
 
 
-def side(layout, q, mid_ref, side_ref, other, par_ref, work):
+def side(layout, q, mid_ref, side_ref, own_table, par_ref, work):
     coef_ref, total_ref, side_par, chunk_ref, s_ref, state_ref = work
     smalls = small_rows(mid_ref)
     far = small_rows(side_ref)
     points = [None, tables(smalls), None]
+    if own_table is not None:
+        points[1][1] = own_table
     points[1 + q] = tables(far)
-    if other is not None:
-        points[1 - q] = tables(small_rows(other))
     rows = gather_rows(chunk_ref, layout, points)
-    off_x, off_y, area, _ = frame(layout, rows[7])
+    off_x, off_y, area, own = frame(layout, rows[7])
     nets = [(p - 1, 0, smalls[p][29:30, 0:LANES]) for p in range(3)]
     nets += [(p - 1, q, far[p][29:30, 0:LANES]) for p in range(3)]
     put_coefs(coef_ref, rows, off_x, off_y, nets, smalls[1])
     spread(far, side_par)
     total_ref[...] = jnp.zeros((8, LANES), F32)
-    for k, c in enumerate(range(3, len(layout))):
+    weights = [mid_ref[2 - p, 0:H, :] for p in range(3)]
+    for k in range(2):
         own_step(
-            total_ref, coef_ref, 1, c, par_ref, mid_ref[1, 0:H, :], k, s_ref, state_ref
+            total_ref, coef_ref, 1, 3 + k, par_ref, weights[1:2], k, s_ref, state_ref
         )
-    for p in (0, 2):
-        near_step(total_ref, coef_ref, p, 3, par_ref, p, mid_ref[p, 0:H, :])
+    near_step(total_ref, coef_ref, 6, 3, par_ref, 3, weights[0::2])
     for p, c in ((0, 0), (1, 0), (1, 1), (2, 1), (1, 2)):
-        near_step(total_ref, coef_ref, 3 + p, c, side_par, p, side_ref[p, 0:H, :])
-    return area, rows[6]
-
-
-def high_kernel(
-    mid_ref, hi_ref, par_ref, coef_ref, info_ref, s_ref, state_ref, side_par, chunk_ref, total_ref
-):
-    work = (coef_ref, total_ref, side_par, chunk_ref, s_ref, state_ref)
-    area, source = side(HIGH, 1, mid_ref, hi_ref, None, par_ref, work)
-    info_ref[0] = total_ref[...]
-    info_ref[1] = area
-    info_ref[2] = source
-
-
-def moved(total, layout):
+        near_step(total_ref, coef_ref, 3 + p, c, side_par, p, [side_ref[2 - p, 0:H, :]])
+    return area, rows[6], own
+
+
+def moved(total, layout, target):
     places = {}
     for c, regions in enumerate(layout[:3]):
         for k, region in enumerate(regions):
             places[region] = (c, SPAN * k)
     rows = []
-    for regions in WINDOW:
+    for regions in target:
         parts = []
         for region in regions:
             if region in places:
@@ -350,81 +350,55 @@
                 parts.append(jnp.zeros((1, SPAN), F32))
         parts += [jnp.zeros((1, SPAN), F32)] * (4 - len(parts))
         rows.append(jnp.concatenate(parts, axis=1))
-    return jnp.concatenate(rows + [jnp.zeros((1, LANES), F32)], axis=0)
-
-
-def last_kernel(
-    mid_ref,
-    lo_ref,
-    hi_ref,
-    w_ref,
-    par_ref,
-    coef_m,
-    info_m,
-    s_m,
-    state_m,
-    coef_h,
-    info_h,
-    s_h,
-    state_h,
-    gw_ref,
-    gs_ref,
-    stat_ref,
-    coef_l,
-    s_l,
-    state_l,
-    side_par,
-    chunk_ref,
-    total_ref,
-    d_ref,
-    acc_ref,
-):
-    work = (coef_l, total_ref, side_par, chunk_ref, s_l, state_l)
-    area_l, source_l = side(BELOW, -1, mid_ref, lo_ref, hi_ref, par_ref, work)
-    below = total_ref[...]
-    high = info_h[0]
-
-    def joined(m, h, l):
-        return jnp.concatenate(
-            [m[0:4], h[3:4], l[3:5], jnp.zeros((1, LANES), F32)], axis=0
-        )
-
-    area = joined(info_m[1], info_h[1], area_l)
-    source = joined(info_m[2], info_h[2], source_l)
-    total = joined(info_m[0], high, below) + moved(high, HIGH) + moved(below, BELOW)
+    return jnp.concatenate(rows + [jnp.zeros((8 - len(rows), LANES), F32)], axis=0)
+
+
+def joined(one, first, last, two):
+    blank = jnp.zeros((6 - (last - first), LANES), F32)
+    return jnp.concatenate([one[first:last], two[3:5], blank], axis=0)
+
+
+def residuals(info_m, first, last, here, total_ref, layout, target):
+    area_s, source_s, own_s = here
+    totals = total_ref[...]
+    area = joined(info_m[1], first, last, area_s)
+    source = joined(info_m[2], first, last, source_s)
+    own = joined(info_m[3], first, last, own_s)
+    total = joined(info_m[0], first, last, totals) + moved(totals, layout, target)
     residual = total - source
-    line = lax.broadcasted_iota(jnp.int32, (8, LANES), 0)
-    own = jnp.where(line < 4, info_m[3], 0.0)
-    loss = jnp.sum(own * area * residual * residual)
     total_ref[...] = 2.0 * area * residual
+    return own * area * residual * residual
+
+
+def put(ref, parts, base):
+    value = functools.reduce(lambda one, two: one + two, parts)
+    ref[...] = value if base is None else base[...] + value
+
+
+def backward(places, groups, total_ref, par_ref, w_ref, d_ref, acc_ref, gw_ref, base):
     w1, w2, pw = par_ref.at[1, 0], par_ref.at[1, 1], par_ref.at[1, 5]
-    places = [(coef_m, c, s_m, state_m, c) for c in range(4)]
-    places += [(coef_h, 3, s_h, state_h, 0), (coef_l, 3, s_l, state_l, 0)]
-    places += [(coef_l, 4, s_l, state_l, 1)]
-
-    def put(ref, parts, first):
-        value = functools.reduce(lambda one, two: one + two, parts)
-        ref[...] = value if first else ref[...] + value
-
-    def cotangents(group, first):
-        base, mix = [], []
-        for row in group:
+
+    def start(k, g):
+        return acc_ref.at[k] if g else None if base is None else base[0].at[k]
+
+    def cotangents(g):
+        d_bases, mixes = [], []
+        for row in groups[g]:
             coef_ref, c, _, state_ref, k = places[row]
             c3 = coef_ref[1, 5, c : c + 1, :]
             adjoint = total_ref[row : row + 1, :]
             scale = state_ref[k, 2] * adjoint
             d_base = scale * state_ref[k, 3]
-            base.append(d_base)
-            mix.append(state_ref[k, 1] * adjoint)
+            d_bases.append(d_base)
+            mixes.append(state_ref[k, 1] * adjoint)
             d_ref[row, :, 0:LANES] = d_base.astype(BF16)
             d_ref[row, :, LANES : 2 * LANES] = (scale * state_ref[k, 4]).astype(BF16)
             d_ref[row, :, 2 * LANES : 3 * LANES] = (scale * state_ref[k, 5]).astype(BF16)
             d_ref[row, :, 3 * LANES :] = (scale * c3).astype(BF16)
-        put(acc_ref.at[4], base, first)
-        put(acc_ref.at[5], mix, first)
-
-    groups = ((0, 1), (2, 3), (4, 5), (6,))
-    cotangents(groups[0], True)
+        put(acc_ref.at[4], d_bases, start(4, g))
+        put(acc_ref.at[5], mixes, start(5, g))
+
+    cotangents(0)
     for g, group in enumerate(groups):
         d_streams = [
             jnp.dot(w_ref[0, 0], d_ref[row], preferred_element_type=F32) for row in group
@@ -439,8 +413,8 @@
             for row in group
         ]
         if g + 1 < len(groups):
-            cotangents(groups[g + 1], False)
-        put(gw_ref, terms, g == 0)
+            cotangents(g + 1)
+        put(gw_ref, terms, gw_ref if g else None if base is None else base[1])
         parts = [[], [], [], []]
         for row, ds in zip(group, d_streams):
             coef_ref, c, _, state_ref, k = places[row]
@@ -457,13 +431,81 @@
             parts[2].append(d_pre)
             parts[3].append(h1 * d1 * ds3)
         for k, part in enumerate(parts):
-            put(acc_ref.at[k], part, g == 0)
+            put(acc_ref.at[k], part, start(k, g))
+
+
+def high_kernel(
+    mid_ref,
+    hi_ref,
+    tab_ref,
+    w_ref,
+    par_ref,
+    coef_m,
+    info_m,
+    s_m,
+    state_m,
+    acc_ref,
+    gw_ref,
+    loss_ref,
+    coef_ref,
+    s_ref,
+    state_ref,
+    side_par,
+    chunk_ref,
+    total_ref,
+    d_ref,
+):
+    work = (coef_ref, total_ref, side_par, chunk_ref, s_ref, state_ref)
+    here = side(HIGH, 1, mid_ref, hi_ref, tab_ref[...], par_ref, work)
+    loss_ref[...] = residuals(info_m, 0, 2, here, total_ref, HIGH, EARLY)
+    places = [(coef_m, c, s_m, state_m, c) for c in range(2)]
+    places += [(coef_ref, 3 + k, s_ref, state_ref, k) for k in range(2)]
+    backward(
+        places, ((0, 1), (2, 3)), total_ref, par_ref, w_ref, d_ref, acc_ref, gw_ref, None
+    )
+
+
+def last_kernel(
+    mid_ref,
+    lo_ref,
+    w_ref,
+    par_ref,
+    coef_m,
+    info_m,
+    s_m,
+    state_m,
+    acc_h,
+    gw_h,
+    loss_h,
+    gw_ref,
+    gs_ref,
+    stat_ref,
+    coef_ref,
+    s_ref,
+    state_ref,
+    side_par,
+    chunk_ref,
+    total_ref,
+    d_ref,
+    acc_ref,
+):
+    work = (coef_ref, total_ref, side_par, chunk_ref, s_ref, state_ref)
+    here = side(BELOW, -1, mid_ref, lo_ref, None, par_ref, work)
+    loss = jnp.sum(
+        loss_h[...] + residuals(info_m, 2, 3, here, total_ref, BELOW, LATE)
+    )
+    places = [(coef_m, 2, s_m, state_m, 2)]
+    places += [(coef_ref, 3 + k, s_ref, state_ref, k) for k in range(2)]
+    base = (acc_h, gw_h)
+    backward(
+        places, ((0, 1), (2,)), total_ref, par_ref, w_ref, d_ref, acc_ref, gw_ref, base
+    )
     sums = [jnp.sum(acc_ref[k], axis=1, keepdims=True) for k in range(6)]
     turn = -16.0 * sums[3]
     grid = jnp.concatenate(
         [
-            sums[0] + turn * w1[:, 0:1],
-            sums[1] + turn * w2[:, 0:1],
+            sums[0] + turn * par_ref[1, 0, :, 0:1],
+            sums[1] + turn * par_ref[1, 1, :, 0:1],
             sums[2],
             sums[4],
             sums[5],
@@ -471,10 +513,9 @@
         ],
         axis=1,
     )
-    gs = jnp.transpose(grid)
-    gs_ref[...] = gs
+    gs_ref[...] = jnp.transpose(grid)
     gw = gw_ref[...]
-    square = jnp.sum(gw * gw) + jnp.sum(gs * gs)
+    square = jnp.sum(gw * gw) + jnp.sum(grid * grid)
     lane = lax.broadcasted_iota(jnp.int32, stat_ref.shape, 2)
     stat_ref[...] = jnp.where(lane == 0, square, jnp.where(lane == 1, loss, 0.0))
 
@@ -559,7 +600,7 @@
     forth = [(i, i + 1) for i in range(count_x - 1)]
     after = lax.ppermute(payload, GX, [(j, i) for i, j in forth])
     before = lax.ppermute(payload, GX, forth)
-    row = jnp.stack([before, payload, after])
+    row = jnp.stack([after, payload, before])
     pairs = [(i, i ^ 1) for i in range(count_y)]
     bonds = [(i, (i + 1) % count_y) for i in range(1, count_y, 2)]
     above = lax.ppermute(row, GY, pairs)
@@ -570,38 +611,41 @@
     def kept(chunks):
         return ((chunks, H, 4 * LANES), BF16), ((chunks, 6, H, LANES), F32)
 
-    def outs(nets, infos, chunks):
-        return (shape((nets, 6, 8, LANES)), shape((infos, 8, LANES))) + tuple(
-            shape(*k) for k in kept(chunks)
-        )
-
     chunk = pltpu.VMEM((8, 8, LANES), F32)
     total = pltpu.VMEM((8, LANES), F32)
-    spreads = (3, 6, H, LANES)
+    accs = (6, H, LANES)
     params, *middle = call(
-        middle_kernel, (shape(spreads),) + outs(3, 4, 4), (chunk, total), flops=10**9
+        middle_kernel,
+        (shape((4, 6, H, LANES)), shape((4, 6, 8, LANES)), shape((4, 8, LANES)))
+        + tuple(shape(*k) for k in kept(3)),
+        (chunk, total),
+        flops=10**9,
     )(row, table)
+
+    def scratch(chunks):
+        return (
+            pltpu.VMEM((7, 6, 8, LANES), F32),
+            *(pltpu.VMEM(*k) for k in kept(2)),
+            pltpu.VMEM((3, 6, H, LANES), F32),
+            chunk,
+            total,
+            pltpu.VMEM((chunks, H, 4 * LANES), BF16),
+        )
+
     high = call(
         high_kernel,
-        outs(6, 3, 1),
-        (pltpu.VMEM(spreads, F32), chunk, total),
+        (shape(accs), shape((H, H)), shape((8, LANES))),
+        scratch(4),
+        limit=20 << 20,
         flops=10**9,
-    )(row, above, params)
+    )(row, above, table, mid_weight, params, *middle)
     grad_w, grad_s, stat = call(
         last_kernel,
         (shape((H, H)), shape((8, H)), shape((first, 1, LANES))),
-        (
-            pltpu.VMEM((6, 6, 8, LANES), F32),
-            *(pltpu.VMEM(*k) for k in kept(2)),
-            pltpu.VMEM(spreads, F32),
-            chunk,
-            total,
-            pltpu.VMEM((7, H, 4 * LANES), BF16),
-            pltpu.VMEM((6, H, LANES), F32),
-        ),
-        limit=24 << 20,
+        scratch(3) + (pltpu.VMEM(accs, F32),),
+        limit=20 << 20,
         flops=10**9,
-    )(row, below, above, mid_weight, params, *middle, *high)
+    )(row, below, mid_weight, params, *middle, *high)
     got = lax.all_to_all(stat, FIRST, 0, 0, tiled=True)
     part = call(sum_kernel, shape((second, 1, LANES)))(got)
     got = lax.all_to_all(part, SECOND, 0, 0, tiled=True)

time: 75.9 us -> 74.5 us (0.982)
  waiting for transfers between devices: 9.66 us -> 7.89 us
    ppermute x1, waiting for transfers between devices: 4.08 us -> 2.18 us  [local(): below = lax.ppermute(row, GY, bonds + [(j, i) for i, j in bonds])]
    pallas_call x2, Pallas kernels: 3.69 us -> 5.47 us  [the longest x1 3.63 us: local(): call(high_kernel, (shape(accs), shape((H, H)), shape((8, LANES))), scratc...]
    pallas_call x1, Pallas kernels: 4.8 us -> 3.45 us  [local(): call(last_kernel, (shape((H, H)), shape((8, H)), shape((first, 1, LANES))...]
  transfers between devices with their start and end apart: 4 -> 4, of which waited for: 4 -> 4; matrix products, arithmetic and copies ran while one was open for 0% -> 0% of each run, Pallas kernels for 5% -> 7%
where the time goes in v4:
time: 74.5 us; the launch traced here: 74.2 us
  blocking collectives  35.5 us (48%)
  starting transfers between devices  19.2 us (26%)
  Pallas kernels  10.9 us (15%)
  waiting for transfers between devices  7.89 us (11%)
    all_to_all x1, blocking collectives, local(): got = lax.all_to_all(stat, FIRST, 0, 0, tiled=True)  22.5 us
    all_to_all x1, blocking collectives, local(): got = lax.all_to_all(part, SECOND, 0, 0, tiled=True)  12.9 us
    ppermute x1, starting transfers between devices, local(): after = lax.ppermute(payload, GX, [(j, i) for i, j in forth])  8.79 us
    ppermute x1, starting transfers between devices, local(): below = lax.ppermute(row, GY, bonds + [(j, i) for i, j in bonds])  5.29 us
    pallas_call x1, Pallas kernels, local(): call(high_kernel, (shape(accs), shape((H, H)), shape((8, LANES))), scratc...  3.63 us
    pallas_call x1, Pallas kernels, local(): call(last_kernel, (shape((H, H)), shape((8, H)), shape((first, 1, LANES))...  3.45 us
    ppermute x1, starting transfers between devices, local(): above = lax.ppermute(row, GY, pairs)  3.12 us
    ppermute x1, waiting for transfers between devices, local(): above = lax.ppermute(row, GY, pairs)  2.62 us
  transfers between devices with their start and end apart: 4, of which 4 were waited for; matrix products, arithmetic and copies ran while one was open for 0% of the time, Pallas kernels for 7%

profile of v4, /device:TPU:1, one launch (start us, length us, event | category | flops | bytes accessed | tf_op | source)
XLA Modules:
  0.0 74.2 jit_solution(13844061091727867556)
XLA Ops:
  0.6 0.0 copy-start
  0.6 1.2 %shard_map.145 = (bf16[288,256]{1,0:T(8,128)(2,1)S(1)}, f32[8,384]{1,0:T(8,128)S(1)}) custom-call(f32[3,3,2,32]{3,2,1,0:T(2,128)} %bitcast.9, f32[3,3,32]{2,1,0:T(4,128)} %refs_1_.1, f32[3,3,2,32]{3,2,1,0:T(2,128)} %bitcast.10, f32[3,3,32]{2,1,0:T(4,128)} %refs_3_.1, f32[3,3,32]{2,1,0:T(4,128)} %refs_4_.1, bf16[1,1,2,256]{3,2,1,0:T(2,128)(2,1)} %refs_5_.1, ...), custom_call_target="tpu_custom_call" | custom-call | bytes 262144 | tf_op jit(solution)/shard_map/pallas_call | solution.py:592
  1.8 8.8 %collective-permute-start = (bf16[288,256]{1,0:T(8,128)(2,1)S(1)}, bf16[288,256]{1,0:T(8,128)(2,1)S(1)}, u32[]{:S(2)}, u32[]{:S(2)}) collective-permute-start(bf16[288,256]{1,0:T(8,128)(2,1)S(1)} %get-tuple-element.25), channel_id=1, source_target_pairs={{16,0},{32,16},{48,32},{64,48},{80,64},{96,80},{112,96},{128,112},... | collective-permute-start | bytes 442376 | tf_op jit(solution)/shard_map/ppermute | solution.py:601
  10.6 2.0 %collective-permute-start.1 = (bf16[288,256]{1,0:T(8,128)(2,1)S(1)}, bf16[288,256]{1,0:T(8,128)(2,1)S(1)}, u32[]{:S(2)}, u32[]{:S(2)}) collective-permute-start(bf16[288,256]{1,0:T(8,128)(2,1)S(1)} %get-tuple-element.25), channel_id=1, source_target_pairs={{0,16},{16,32},{32,48},{48,64},{64,80},{80,96},{96,112},{112,128},... | collective-permute-start | bytes 442376 | tf_op jit(solution)/shard_map/ppermute | solution.py:602
  12.6 1.0 %collective-permute-done = bf16[288,256]{1,0:T(8,128)(2,1)S(1)} collective-permute-done((bf16[288,256]{1,0:T(8,128)(2,1)S(1)}, bf16[288,256]{1,0:T(8,128)(2,1)S(1)}, u32[]{:S(2)}, u32[]{:S(2)}) %collective-permute-start) | collective-permute-done | bytes 147488 | tf_op jit(solution)/shard_map/ppermute | solution.py:601
  13.6 2.1 %collective-permute-done.1 = bf16[288,256]{1,0:T(8,128)(2,1)S(1)} collective-permute-done((bf16[288,256]{1,0:T(8,128)(2,1)S(1)}, bf16[288,256]{1,0:T(8,128)(2,1)S(1)}, u32[]{:S(2)}, u32[]{:S(2)}) %collective-permute-start.1) | collective-permute-done | bytes 147488 | tf_op jit(solution)/shard_map/ppermute | solution.py:602
  15.7 0.1 pad_maximum_fusion.mid_ref
  15.7 3.1 %collective-permute-start.3 = (bf16[3,288,256]{2,1,0:T(8,128)(2,1)S(1)}, bf16[3,288,256]{2,1,0:T(8,128)(2,1)S(1)}, u32[]{:S(2)}, u32[]{:S(2)}) collective-permute-start(bf16[3,288,256]{2,1,0:T(8,128)(2,1)S(1)} %pad_maximum_fusion.mid_ref), channel_id=1, source_target_pairs={{0,1},{1,0},{2,3},{3,2},{4,5},{5,4},{6,7},{7,6},{8,9},{9,8},{10,11... | collective-permute-start | bytes 1327112 | tf_op jit(solution)/shard_map/ppermute | solution.py:606
  18.9 5.3 %collective-permute-start.2 = (bf16[3,288,256]{2,1,0:T(8,128)(2,1)S(1)}, bf16[3,288,256]{2,1,0:T(8,128)(2,1)S(1)}, u32[]{:S(2)}, u32[]{:S(2)}) collective-permute-start(bf16[3,288,256]{2,1,0:T(8,128)(2,1)S(1)} %pad_maximum_fusion.mid_ref), channel_id=1, source_target_pairs={{1,2},{3,4},{5,6},{7,8},{9,10},{11,12},{13,14},{15,0},{2,1},{4,3},... | collective-permute-start | bytes 1327112 | tf_op jit(solution)/shard_map/ppermute | solution.py:607
  24.2 1.8 %shard_map.146 = (f32[4,6,256,128]{3,2,1,0:T(8,128)S(1)}, f32[4,6,8,128]{3,2,1,0:T(8,128)S(1)}, f32[4,8,128]{2,1,0:T(8,128)S(1)}, bf16[3,256,512]{2,1,0:T(8,128)(2,1)S(1)}, f32[3,6,256,128]{3,2,1,0:T(8,128)S(1)}) custom-call(bf16[3,288,256]{2,1,0:T(8,128)(2,1)S(1)} %pad_maximum_fusion.mid_ref, f32[8,384]{1,0:T(8,128)S(1)} %get-tuple-element.26.tab_ref), custom_call_target="tpu_custom_call" | custom-call | flops 1000000000 | bytes 262144 | tf_op jit(solution)/shard_map/pallas_call | solution.py:617
  26.0 2.6 %collective-permute-done.3.hi_ref = bf16[3,288,256]{2,1,0:T(8,128)(2,1)S(1)} collective-permute-done((bf16[3,288,256]{2,1,0:T(8,128)(2,1)S(1)}, bf16[3,288,256]{2,1,0:T(8,128)(2,1)S(1)}, u32[]{:S(2)}, u32[]{:S(2)}) %collective-permute-start.3) | collective-permute-done | bytes 442400 | tf_op jit(solution)/shard_map/ppermute | solution.py:606
  28.6 0.0 copy-done
  28.6 3.6 %shard_map.147 = (f32[6,256,128]{2,1,0:T(8,128)S(1)}, f32[256,256]{1,0:T(8,128)S(1)}, f32[8,128]{1,0:T(8,128)S(1)}) custom-call(bf16[3,288,256]{2,1,0:T(8,128)(2,1)S(1)} %pad_maximum_fusion.mid_ref, bf16[3,288,256]{2,1,0:T(8,128)(2,1)S(1)} %collective-permute-done.3.hi_ref, f32[8,384]{1,0:T(8,128)S(1)} %get-tuple-element.26.tab_ref, ...), custom_call_target="tpu_custom_call" | custom-call | flops 1000000000 | bytes 262144 | tf_op jit(solution)/shard_map/pallas_call | solution.py:635
  32.3 2.2 %collective-permute-done.2.lo_ref = bf16[3,288,256]{2,1,0:T(8,128)(2,1)S(1)} collective-permute-done((bf16[3,288,256]{2,1,0:T(8,128)(2,1)S(1)}, bf16[3,288,256]{2,1,0:T(8,128)(2,1)S(1)}, u32[]{:S(2)}, u32[]{:S(2)}) %collective-permute-start.2) | collective-permute-done | bytes 442400 | tf_op jit(solution)/shard_map/ppermute | solution.py:607
  34.5 3.5 %shard_map.148 = (f32[256,256]{1,0:T(8,128)S(1)}, f32[8,256]{1,0:T(8,128)S(1)}, f32[16,1,128]{2,1,0:T(1,128)S(1)}) custom-call(bf16[3,288,256]{2,1,0:T(8,128)(2,1)S(1)} %pad_maximum_fusion.mid_ref, bf16[3,288,256]{2,1,0:T(8,128)(2,1)S(1)} %collective-permute-done.2.lo_ref, bf16[1,1,256,256]{3,2,1,0:T(8,128)(2,1)S(1)} %copy-done, ...), custom_call_target="tpu_custom_call" | custom-call | flops 1000000000 | bytes 262144 | tf_op jit(solution)/shard_map/pallas_call | solution.py:642
  37.9 22.5 %all_to_all.10.got_ref = f32[16,1,128]{2,1,0:T(1,128)S(1)} all-to-all(f32[16,1,128]{2,1,0:T(1,128)S(1)} %get-tuple-element.35), channel_id=1, replica_groups=mesh['z'=8,'yh'=2,'c'=2,'yl'=4,'x'=4] {'z','c'}, dimensions={0} | all-to-all | bytes 16384 | tf_op jit(solution)/shard_map/all_to_all | solution.py:649
  60.5 12.9 %all_to_all.11.refs_0_ = f32[32,1,128]{2,1,0:T(1,128)S(1)} all-to-all(f32[32,1,128]{2,1,0:T(1,128)S(1)} %shard_map.149), channel_id=1, replica_groups=mesh['z'=8,'yh'=2,'c'=2,'yl'=4,'x'=4] {'yh','yl','x'}, dimensions={0} | all-to-all | bytes 32768 | tf_op jit(solution)/shard_map/all_to_all | solution.py:651
  73.4 0.8 %shard_map.150 = (f32[1,1,2,256]{3,2,1,0:T(2,128)}, f32[1,1,256]{2,1,0:T(1,128)}, f32[1,1,256,256]{3,2,1,0:T(8,128)}, f32[1,1,256]{2,1,0:T(1,128)}, f32[1,1,256]{2,1,0:T(1,128)}, /*index=5*/f32[1,1]{1,0:T(1,128)}) custom-call(f32[32,1,128]{2,1,0:T(1,128)S(1)} %all_to_all.11.refs_0_, f32[256,256]{1,0:T(8,128)S(1)} %get-tuple-element.36.refs_1_, ...), custom_call_target="tpu_custom_call" | custom-call | bytes 262144 | tf_op jit(solution)/shard_map/pallas_call | solution.py:652
  (1 shorter events, 0.0 us)
Async XLA Ops:
  0.6 28.0 %copy-start = (bf16[1,1,256,256]{3,2,1,0:T(8,128)(2,1)S(1)}, bf16[1,1,256,256]{3,2,1,0:T(8,128)(2,1)}, u32[]{:S(2)}) copy-start(bf16[1,1,256,256]{3,2,1,0:T(8,128)(2,1)} %w_ref.3) | copy-start | bytes 393220
  1.8 11.8 %collective-permute-start = (bf16[288,256]{1,0:T(8,128)(2,1)S(1)}, bf16[288,256]{1,0:T(8,128)(2,1)S(1)}, u32[]{:S(2)}, u32[]{:S(2)}) collective-permute-start(bf16[288,256]{1,0:T(8,128)(2,1)S(1)} %get-tuple-element.25), channel_id=1, source_target_pairs={{16,0},{32,16},{48,32},{64,48},{80,64},{96,80},{112,96},{128,112},... | collective-permute-start | bytes 442376 | tf_op jit(solution)/shard_map/ppermute | solution.py:601
  10.6 5.1 %collective-permute-start.1 = (bf16[288,256]{1,0:T(8,128)(2,1)S(1)}, bf16[288,256]{1,0:T(8,128)(2,1)S(1)}, u32[]{:S(2)}, u32[]{:S(2)}) collective-permute-start(bf16[288,256]{1,0:T(8,128)(2,1)S(1)} %get-tuple-element.25), channel_id=1, source_target_pairs={{0,16},{16,32},{32,48},{48,64},{64,80},{80,96},{96,112},{112,128},... | collective-permute-start | bytes 442376 | tf_op jit(solution)/shard_map/ppermute | solution.py:602
  15.7 12.9 %collective-permute-start.3 = (bf16[3,288,256]{2,1,0:T(8,128)(2,1)S(1)}, bf16[3,288,256]{2,1,0:T(8,128)(2,1)S(1)}, u32[]{:S(2)}, u32[]{:S(2)}) collective-permute-start(bf16[3,288,256]{2,1,0:T(8,128)(2,1)S(1)} %pad_maximum_fusion.mid_ref), channel_id=1, source_target_pairs={{0,1},{1,0},{2,3},{3,2},{4,5},{5,4},{6,7},{7,6},{8,9},{9,8},{10,11... | collective-permute-start | bytes 1327112 | tf_op jit(solution)/shard_map/ppermute | solution.py:606
  18.9 15.6 %collective-permute-start.2 = (bf16[3,288,256]{2,1,0:T(8,128)(2,1)S(1)}, bf16[3,288,256]{2,1,0:T(8,128)(2,1)S(1)}, u32[]{:S(2)}, u32[]{:S(2)}) collective-permute-start(bf16[3,288,256]{2,1,0:T(8,128)(2,1)S(1)} %pad_maximum_fusion.mid_ref), channel_id=1, source_target_pairs={{1,2},{3,4},{5,6},{7,8},{9,10},{11,12},{13,14},{15,0},{2,1},{4,3},... | collective-permute-start | bytes 1327112 | tf_op jit(solution)/shard_map/ppermute | solution.py:607

commit v5 on v4

--- a/solution.py
+++ b/solution.py
@@ -372,7 +372,9 @@
 
 def put(ref, parts, base):
     value = functools.reduce(lambda one, two: one + two, parts)
-    ref[...] = value if base is None else base[...] + value
+    value = value if base is None else base[...] + value
+    ref[...] = value
+    return value
 
 
 def backward(places, groups, total_ref, par_ref, w_ref, d_ref, acc_ref, gw_ref, base):
@@ -414,7 +416,8 @@
         ]
         if g + 1 < len(groups):
             cotangents(g + 1)
-        put(gw_ref, terms, gw_ref if g else None if base is None else base[1])
+        grad_w = put(gw_ref, terms, gw_ref if g else None if base is None else base[1])
+        norm = jnp.sum(grad_w * grad_w)
         parts = [[], [], [], []]
         for row, ds in zip(group, d_streams):
             coef_ref, c, _, state_ref, k = places[row]
@@ -432,6 +435,7 @@
             parts[3].append(h1 * d1 * ds3)
         for k, part in enumerate(parts):
             put(acc_ref.at[k], part, start(k, g))
+    return norm
 
 
 def high_kernel(
@@ -497,8 +501,8 @@
     places = [(coef_m, 2, s_m, state_m, 2)]
     places += [(coef_ref, 3 + k, s_ref, state_ref, k) for k in range(2)]
     base = (acc_h, gw_h)
-    backward(
-        places, ((0, 1), (2,)), total_ref, par_ref, w_ref, d_ref, acc_ref, gw_ref, base
+    norm = backward(
+        places, ((0, 1, 2),), total_ref, par_ref, w_ref, d_ref, acc_ref, gw_ref, base
     )
     sums = [jnp.sum(acc_ref[k], axis=1, keepdims=True) for k in range(6)]
     turn = -16.0 * sums[3]
@@ -514,8 +518,7 @@
         axis=1,
     )
     gs_ref[...] = jnp.transpose(grid)
-    gw = gw_ref[...]
-    square = jnp.sum(gw * gw) + jnp.sum(grid * grid)
+    square = norm + jnp.sum(grid * grid)
     lane = lax.broadcasted_iota(jnp.int32, stat_ref.shape, 2)
     stat_ref[...] = jnp.where(lane == 0, square, jnp.where(lane == 1, loss, 0.0))
 
@@ -528,10 +531,11 @@
 def scale_kernel(nets, got_ref, gw_ref, gs_ref, o0, o1, o2, o3, o4, loss_ref):
     total = jnp.sum(got_ref[...], axis=0)
     rms = jnp.sqrt(total[:, 0:1] / (nets * (H * H + 5 * H)) + EPS)
-    gs = gs_ref[...] / rms
+    inverse = 1.0 / rms
+    gs = gs_ref[...] * inverse
     o0[0, 0] = gs[0:2]
     o1[0] = gs[2:3]
-    o2[0, 0] = gw_ref[...] / rms
+    o2[0, 0] = gw_ref[...] * inverse
     o3[0] = gs[3:4]
     o4[0] = gs[4:5]
     loss_ref[...] = total[:, 1:2]

time: 74.5 us -> 74.5 us (level)
  no operation moved by 1% of the time
where the time goes in v5:
time: 74.5 us; the launch traced here: 74.3 us
  blocking collectives  35.5 us (48%)
  starting transfers between devices  19.2 us (26%)
  Pallas kernels  11 us (15%)
  waiting for transfers between devices  7.89 us (11%)
    all_to_all x1, blocking collectives, local(): got = lax.all_to_all(stat, FIRST, 0, 0, tiled=True)  22.5 us
    all_to_all x1, blocking collectives, local(): got = lax.all_to_all(part, SECOND, 0, 0, tiled=True)  12.9 us
    ppermute x1, starting transfers between devices, local(): after = lax.ppermute(payload, GX, [(j, i) for i, j in forth])  8.79 us
    ppermute x1, starting transfers between devices, local(): below = lax.ppermute(row, GY, bonds + [(j, i) for i, j in bonds])  5.29 us
    pallas_call x1, Pallas kernels, local(): call(high_kernel, (shape(accs), shape((H, H)), shape((8, LANES))), scratc...  3.63 us
    pallas_call x1, Pallas kernels, local(): call(last_kernel, (shape((H, H)), shape((8, H)), shape((first, 1, LANES))...  3.48 us
    ppermute x1, starting transfers between devices, local(): above = lax.ppermute(row, GY, pairs)  3.12 us
    ppermute x1, waiting for transfers between devices, local(): above = lax.ppermute(row, GY, pairs)  2.62 us
  transfers between devices with their start and end apart: 4, of which 4 were waited for; matrix products, arithmetic and copies ran while one was open for 0% of the time, Pallas kernels for 7%

profile of v5, /device:TPU:1, one launch (start us, length us, event | category | flops | bytes accessed | tf_op | source)
XLA Modules:
  0.0 74.3 jit_solution(4767528478745267253)
XLA Ops:
  0.6 0.0 copy-start
  0.6 1.2 %shard_map.145 = (bf16[288,256]{1,0:T(8,128)(2,1)S(1)}, f32[8,384]{1,0:T(8,128)S(1)}) custom-call(f32[3,3,2,32]{3,2,1,0:T(2,128)} %bitcast.9, f32[3,3,32]{2,1,0:T(4,128)} %refs_1_.1, f32[3,3,2,32]{3,2,1,0:T(2,128)} %bitcast.10, f32[3,3,32]{2,1,0:T(4,128)} %refs_3_.1, f32[3,3,32]{2,1,0:T(4,128)} %refs_4_.1, bf16[1,1,2,256]{3,2,1,0:T(2,128)(2,1)} %refs_5_.1, ...), custom_call_target="tpu_custom_call" | custom-call | bytes 262144 | tf_op jit(solution)/shard_map/pallas_call | solution.py:596
  1.8 8.8 %collective-permute-start = (bf16[288,256]{1,0:T(8,128)(2,1)S(1)}, bf16[288,256]{1,0:T(8,128)(2,1)S(1)}, u32[]{:S(2)}, u32[]{:S(2)}) collective-permute-start(bf16[288,256]{1,0:T(8,128)(2,1)S(1)} %get-tuple-element.25), channel_id=1, source_target_pairs={{16,0},{32,16},{48,32},{64,48},{80,64},{96,80},{112,96},{128,112},... | collective-permute-start | bytes 442376 | tf_op jit(solution)/shard_map/ppermute | solution.py:605
  10.6 2.0 %collective-permute-start.1 = (bf16[288,256]{1,0:T(8,128)(2,1)S(1)}, bf16[288,256]{1,0:T(8,128)(2,1)S(1)}, u32[]{:S(2)}, u32[]{:S(2)}) collective-permute-start(bf16[288,256]{1,0:T(8,128)(2,1)S(1)} %get-tuple-element.25), channel_id=1, source_target_pairs={{0,16},{16,32},{32,48},{48,64},{64,80},{80,96},{96,112},{112,128},... | collective-permute-start | bytes 442376 | tf_op jit(solution)/shard_map/ppermute | solution.py:606
  12.6 1.0 %collective-permute-done = bf16[288,256]{1,0:T(8,128)(2,1)S(1)} collective-permute-done((bf16[288,256]{1,0:T(8,128)(2,1)S(1)}, bf16[288,256]{1,0:T(8,128)(2,1)S(1)}, u32[]{:S(2)}, u32[]{:S(2)}) %collective-permute-start) | collective-permute-done | bytes 147488 | tf_op jit(solution)/shard_map/ppermute | solution.py:605
  13.6 2.1 %collective-permute-done.1 = bf16[288,256]{1,0:T(8,128)(2,1)S(1)} collective-permute-done((bf16[288,256]{1,0:T(8,128)(2,1)S(1)}, bf16[288,256]{1,0:T(8,128)(2,1)S(1)}, u32[]{:S(2)}, u32[]{:S(2)}) %collective-permute-start.1) | collective-permute-done | bytes 147488 | tf_op jit(solution)/shard_map/ppermute | solution.py:606
  15.7 0.1 pad_maximum_fusion.mid_ref
  15.7 3.1 %collective-permute-start.3 = (bf16[3,288,256]{2,1,0:T(8,128)(2,1)S(1)}, bf16[3,288,256]{2,1,0:T(8,128)(2,1)S(1)}, u32[]{:S(2)}, u32[]{:S(2)}) collective-permute-start(bf16[3,288,256]{2,1,0:T(8,128)(2,1)S(1)} %pad_maximum_fusion.mid_ref), channel_id=1, source_target_pairs={{0,1},{1,0},{2,3},{3,2},{4,5},{5,4},{6,7},{7,6},{8,9},{9,8},{10,11... | collective-permute-start | bytes 1327112 | tf_op jit(solution)/shard_map/ppermute | solution.py:610
  18.9 5.3 %collective-permute-start.2 = (bf16[3,288,256]{2,1,0:T(8,128)(2,1)S(1)}, bf16[3,288,256]{2,1,0:T(8,128)(2,1)S(1)}, u32[]{:S(2)}, u32[]{:S(2)}) collective-permute-start(bf16[3,288,256]{2,1,0:T(8,128)(2,1)S(1)} %pad_maximum_fusion.mid_ref), channel_id=1, source_target_pairs={{1,2},{3,4},{5,6},{7,8},{9,10},{11,12},{13,14},{15,0},{2,1},{4,3},... | collective-permute-start | bytes 1327112 | tf_op jit(solution)/shard_map/ppermute | solution.py:611
  24.2 1.8 %shard_map.146 = (f32[4,6,256,128]{3,2,1,0:T(8,128)S(1)}, f32[4,6,8,128]{3,2,1,0:T(8,128)S(1)}, f32[4,8,128]{2,1,0:T(8,128)S(1)}, bf16[3,256,512]{2,1,0:T(8,128)(2,1)S(1)}, f32[3,6,256,128]{3,2,1,0:T(8,128)S(1)}) custom-call(bf16[3,288,256]{2,1,0:T(8,128)(2,1)S(1)} %pad_maximum_fusion.mid_ref, f32[8,384]{1,0:T(8,128)S(1)} %get-tuple-element.26.tab_ref), custom_call_target="tpu_custom_call" | custom-call | flops 1000000000 | bytes 262144 | tf_op jit(solution)/shard_map/pallas_call | solution.py:621
  26.0 2.6 %collective-permute-done.3.hi_ref = bf16[3,288,256]{2,1,0:T(8,128)(2,1)S(1)} collective-permute-done((bf16[3,288,256]{2,1,0:T(8,128)(2,1)S(1)}, bf16[3,288,256]{2,1,0:T(8,128)(2,1)S(1)}, u32[]{:S(2)}, u32[]{:S(2)}) %collective-permute-start.3) | collective-permute-done | bytes 442400 | tf_op jit(solution)/shard_map/ppermute | solution.py:610
  28.6 0.0 copy-done
  28.6 3.6 %shard_map.147 = (f32[6,256,128]{2,1,0:T(8,128)S(1)}, f32[256,256]{1,0:T(8,128)S(1)}, f32[8,128]{1,0:T(8,128)S(1)}) custom-call(bf16[3,288,256]{2,1,0:T(8,128)(2,1)S(1)} %pad_maximum_fusion.mid_ref, bf16[3,288,256]{2,1,0:T(8,128)(2,1)S(1)} %collective-permute-done.3.hi_ref, f32[8,384]{1,0:T(8,128)S(1)} %get-tuple-element.26.tab_ref, ...), custom_call_target="tpu_custom_call" | custom-call | flops 1000000000 | bytes 262144 | tf_op jit(solution)/shard_map/pallas_call | solution.py:639
  32.3 2.2 %collective-permute-done.2.lo_ref = bf16[3,288,256]{2,1,0:T(8,128)(2,1)S(1)} collective-permute-done((bf16[3,288,256]{2,1,0:T(8,128)(2,1)S(1)}, bf16[3,288,256]{2,1,0:T(8,128)(2,1)S(1)}, u32[]{:S(2)}, u32[]{:S(2)}) %collective-permute-start.2) | collective-permute-done | bytes 442400 | tf_op jit(solution)/shard_map/ppermute | solution.py:611
  34.5 3.5 %shard_map.148 = (f32[256,256]{1,0:T(8,128)S(1)}, f32[8,256]{1,0:T(8,128)S(1)}, f32[16,1,128]{2,1,0:T(1,128)S(1)}) custom-call(bf16[3,288,256]{2,1,0:T(8,128)(2,1)S(1)} %pad_maximum_fusion.mid_ref, bf16[3,288,256]{2,1,0:T(8,128)(2,1)S(1)} %collective-permute-done.2.lo_ref, bf16[1,1,256,256]{3,2,1,0:T(8,128)(2,1)S(1)} %copy-done, ...), custom_call_target="tpu_custom_call" | custom-call | flops 1000000000 | bytes 262144 | tf_op jit(solution)/shard_map/pallas_call | solution.py:646
  38.0 22.5 %all_to_all.10.got_ref = f32[16,1,128]{2,1,0:T(1,128)S(1)} all-to-all(f32[16,1,128]{2,1,0:T(1,128)S(1)} %get-tuple-element.35), channel_id=1, replica_groups=mesh['z'=8,'yh'=2,'c'=2,'yl'=4,'x'=4] {'z','c'}, dimensions={0} | all-to-all | bytes 16384 | tf_op jit(solution)/shard_map/all_to_all | solution.py:653
  60.5 12.9 %all_to_all.11.refs_0_ = f32[32,1,128]{2,1,0:T(1,128)S(1)} all-to-all(f32[32,1,128]{2,1,0:T(1,128)S(1)} %shard_map.149), channel_id=1, replica_groups=mesh['z'=8,'yh'=2,'c'=2,'yl'=4,'x'=4] {'yh','yl','x'}, dimensions={0} | all-to-all | bytes 32768 | tf_op jit(solution)/shard_map/all_to_all | solution.py:655
  73.4 0.8 %shard_map.150 = (f32[1,1,2,256]{3,2,1,0:T(2,128)}, f32[1,1,256]{2,1,0:T(1,128)}, f32[1,1,256,256]{3,2,1,0:T(8,128)}, f32[1,1,256]{2,1,0:T(1,128)}, f32[1,1,256]{2,1,0:T(1,128)}, /*index=5*/f32[1,1]{1,0:T(1,128)}) custom-call(f32[32,1,128]{2,1,0:T(1,128)S(1)} %all_to_all.11.refs_0_, f32[256,256]{1,0:T(8,128)S(1)} %get-tuple-element.36.refs_1_, ...), custom_call_target="tpu_custom_call" | custom-call | bytes 262144 | tf_op jit(solution)/shard_map/pallas_call | solution.py:656
  (1 shorter events, 0.0 us)
Async XLA Ops:
  0.6 28.0 %copy-start = (bf16[1,1,256,256]{3,2,1,0:T(8,128)(2,1)S(1)}, bf16[1,1,256,256]{3,2,1,0:T(8,128)(2,1)}, u32[]{:S(2)}) copy-start(bf16[1,1,256,256]{3,2,1,0:T(8,128)(2,1)} %w_ref.3) | copy-start | bytes 393220
  1.8 11.8 %collective-permute-start = (bf16[288,256]{1,0:T(8,128)(2,1)S(1)}, bf16[288,256]{1,0:T(8,128)(2,1)S(1)}, u32[]{:S(2)}, u32[]{:S(2)}) collective-permute-start(bf16[288,256]{1,0:T(8,128)(2,1)S(1)} %get-tuple-element.25), channel_id=1, source_target_pairs={{16,0},{32,16},{48,32},{64,48},{80,64},{96,80},{112,96},{128,112},... | collective-permute-start | bytes 442376 | tf_op jit(solution)/shard_map/ppermute | solution.py:605
  10.6 5.1 %collective-permute-start.1 = (bf16[288,256]{1,0:T(8,128)(2,1)S(1)}, bf16[288,256]{1,0:T(8,128)(2,1)S(1)}, u32[]{:S(2)}, u32[]{:S(2)}) collective-permute-start(bf16[288,256]{1,0:T(8,128)(2,1)S(1)} %get-tuple-element.25), channel_id=1, source_target_pairs={{0,16},{16,32},{32,48},{48,64},{64,80},{80,96},{96,112},{112,128},... | collective-permute-start | bytes 442376 | tf_op jit(solution)/shard_map/ppermute | solution.py:606
  15.7 12.9 %collective-permute-start.3 = (bf16[3,288,256]{2,1,0:T(8,128)(2,1)S(1)}, bf16[3,288,256]{2,1,0:T(8,128)(2,1)S(1)}, u32[]{:S(2)}, u32[]{:S(2)}) collective-permute-start(bf16[3,288,256]{2,1,0:T(8,128)(2,1)S(1)} %pad_maximum_fusion.mid_ref), channel_id=1, source_target_pairs={{0,1},{1,0},{2,3},{3,2},{4,5},{5,4},{6,7},{7,6},{8,9},{9,8},{10,11... | collective-permute-start | bytes 1327112 | tf_op jit(solution)/shard_map/ppermute | solution.py:610
  18.9 15.6 %collective-permute-start.2 = (bf16[3,288,256]{2,1,0:T(8,128)(2,1)S(1)}, bf16[3,288,256]{2,1,0:T(8,128)(2,1)S(1)}, u32[]{:S(2)}, u32[]{:S(2)}) collective-permute-start(bf16[3,288,256]{2,1,0:T(8,128)(2,1)S(1)} %pad_maximum_fusion.mid_ref), channel_id=1, source_target_pairs={{1,2},{3,4},{5,6},{7,8},{9,10},{11,12},{13,14},{15,0},{2,1},{4,3},... | collective-permute-start | bytes 1327112 | tf_op jit(solution)/shard_map/ppermute | solution.py:611

commit v6 on v4

--- a/solution.py
+++ b/solution.py
@@ -461,7 +461,7 @@
     places = [(coef_m, c, s_m, state_m, c) for c in range(2)]
     places += [(coef_ref, 3 + k, s_ref, state_ref, k) for k in range(2)]
     backward(
-        places, ((0, 1), (2, 3)), total_ref, par_ref, w_ref, d_ref, acc_ref, gw_ref, None
+        places, ((0, 1, 2, 3),), total_ref, par_ref, w_ref, d_ref, acc_ref, gw_ref, None
     )
 
 

time: 74.5 us -> 74.5 us (level)
  no operation moved by 1% of the time
where the time goes in v6:
time: 74.5 us; the launch traced here: 74.2 us
  blocking collectives  35.5 us (48%)
  starting transfers between devices  19.2 us (26%)
  Pallas kernels  11 us (15%)
  waiting for transfers between devices  7.81 us (10%)
    all_to_all x1, blocking collectives, local(): got = lax.all_to_all(stat, FIRST, 0, 0, tiled=True)  22.5 us
    all_to_all x1, blocking collectives, local(): got = lax.all_to_all(part, SECOND, 0, 0, tiled=True)  12.9 us
    ppermute x1, starting transfers between devices, local(): after = lax.ppermute(payload, GX, [(j, i) for i, j in forth])  8.79 us
    ppermute x1, starting transfers between devices, local(): below = lax.ppermute(row, GY, bonds + [(j, i) for i, j in bonds])  5.29 us
    pallas_call x1, Pallas kernels, local(): call(high_kernel, (shape(accs), shape((H, H)), shape((8, LANES))), scratc...  3.72 us
    pallas_call x1, Pallas kernels, local(): call(last_kernel, (shape((H, H)), shape((8, H)), shape((first, 1, LANES))...  3.45 us
    ppermute x1, starting transfers between devices, local(): above = lax.ppermute(row, GY, pairs)  3.12 us
    ppermute x1, waiting for transfers between devices, local(): above = lax.ppermute(row, GY, pairs)  2.62 us
  transfers between devices with their start and end apart: 4, of which 4 were waited for; matrix products, arithmetic and copies ran while one was open for 0% of the time, Pallas kernels for 7%

profile of v6, /device:TPU:1, one launch (start us, length us, event | category | flops | bytes accessed | tf_op | source)
XLA Modules:
  0.0 74.2 jit_solution(9577454856280053297)
XLA Ops:
  0.6 0.0 copy-start
  0.6 1.2 %shard_map.145 = (bf16[288,256]{1,0:T(8,128)(2,1)S(1)}, f32[8,384]{1,0:T(8,128)S(1)}) custom-call(f32[3,3,2,32]{3,2,1,0:T(2,128)} %bitcast.9, f32[3,3,32]{2,1,0:T(4,128)} %refs_1_.1, f32[3,3,2,32]{3,2,1,0:T(2,128)} %bitcast.10, f32[3,3,32]{2,1,0:T(4,128)} %refs_3_.1, f32[3,3,32]{2,1,0:T(4,128)} %refs_4_.1, bf16[1,1,2,256]{3,2,1,0:T(2,128)(2,1)} %refs_5_.1, ...), custom_call_target="tpu_custom_call" | custom-call | bytes 262144 | tf_op jit(solution)/shard_map/pallas_call | solution.py:592
  1.8 8.8 %collective-permute-start = (bf16[288,256]{1,0:T(8,128)(2,1)S(1)}, bf16[288,256]{1,0:T(8,128)(2,1)S(1)}, u32[]{:S(2)}, u32[]{:S(2)}) collective-permute-start(bf16[288,256]{1,0:T(8,128)(2,1)S(1)} %get-tuple-element.25), channel_id=1, source_target_pairs={{16,0},{32,16},{48,32},{64,48},{80,64},{96,80},{112,96},{128,112},... | collective-permute-start | bytes 442376 | tf_op jit(solution)/shard_map/ppermute | solution.py:601
  10.6 2.0 %collective-permute-start.1 = (bf16[288,256]{1,0:T(8,128)(2,1)S(1)}, bf16[288,256]{1,0:T(8,128)(2,1)S(1)}, u32[]{:S(2)}, u32[]{:S(2)}) collective-permute-start(bf16[288,256]{1,0:T(8,128)(2,1)S(1)} %get-tuple-element.25), channel_id=1, source_target_pairs={{0,16},{16,32},{32,48},{48,64},{64,80},{80,96},{96,112},{112,128},... | collective-permute-start | bytes 442376 | tf_op jit(solution)/shard_map/ppermute | solution.py:602
  12.6 1.0 %collective-permute-done = bf16[288,256]{1,0:T(8,128)(2,1)S(1)} collective-permute-done((bf16[288,256]{1,0:T(8,128)(2,1)S(1)}, bf16[288,256]{1,0:T(8,128)(2,1)S(1)}, u32[]{:S(2)}, u32[]{:S(2)}) %collective-permute-start) | collective-permute-done | bytes 147488 | tf_op jit(solution)/shard_map/ppermute | solution.py:601
  13.6 2.1 %collective-permute-done.1 = bf16[288,256]{1,0:T(8,128)(2,1)S(1)} collective-permute-done((bf16[288,256]{1,0:T(8,128)(2,1)S(1)}, bf16[288,256]{1,0:T(8,128)(2,1)S(1)}, u32[]{:S(2)}, u32[]{:S(2)}) %collective-permute-start.1) | collective-permute-done | bytes 147488 | tf_op jit(solution)/shard_map/ppermute | solution.py:602
  15.7 0.1 pad_maximum_fusion.mid_ref
  15.7 3.1 %collective-permute-start.3 = (bf16[3,288,256]{2,1,0:T(8,128)(2,1)S(1)}, bf16[3,288,256]{2,1,0:T(8,128)(2,1)S(1)}, u32[]{:S(2)}, u32[]{:S(2)}) collective-permute-start(bf16[3,288,256]{2,1,0:T(8,128)(2,1)S(1)} %pad_maximum_fusion.mid_ref), channel_id=1, source_target_pairs={{0,1},{1,0},{2,3},{3,2},{4,5},{5,4},{6,7},{7,6},{8,9},{9,8},{10,11... | collective-permute-start | bytes 1327112 | tf_op jit(solution)/shard_map/ppermute | solution.py:606
  18.9 5.3 %collective-permute-start.2 = (bf16[3,288,256]{2,1,0:T(8,128)(2,1)S(1)}, bf16[3,288,256]{2,1,0:T(8,128)(2,1)S(1)}, u32[]{:S(2)}, u32[]{:S(2)}) collective-permute-start(bf16[3,288,256]{2,1,0:T(8,128)(2,1)S(1)} %pad_maximum_fusion.mid_ref), channel_id=1, source_target_pairs={{1,2},{3,4},{5,6},{7,8},{9,10},{11,12},{13,14},{15,0},{2,1},{4,3},... | collective-permute-start | bytes 1327112 | tf_op jit(solution)/shard_map/ppermute | solution.py:607
  24.2 1.8 %shard_map.146 = (f32[4,6,256,128]{3,2,1,0:T(8,128)S(1)}, f32[4,6,8,128]{3,2,1,0:T(8,128)S(1)}, f32[4,8,128]{2,1,0:T(8,128)S(1)}, bf16[3,256,512]{2,1,0:T(8,128)(2,1)S(1)}, f32[3,6,256,128]{3,2,1,0:T(8,128)S(1)}) custom-call(bf16[3,288,256]{2,1,0:T(8,128)(2,1)S(1)} %pad_maximum_fusion.mid_ref, f32[8,384]{1,0:T(8,128)S(1)} %get-tuple-element.26.tab_ref), custom_call_target="tpu_custom_call" | custom-call | flops 1000000000 | bytes 262144 | tf_op jit(solution)/shard_map/pallas_call | solution.py:617
  26.0 2.6 %collective-permute-done.3.hi_ref = bf16[3,288,256]{2,1,0:T(8,128)(2,1)S(1)} collective-permute-done((bf16[3,288,256]{2,1,0:T(8,128)(2,1)S(1)}, bf16[3,288,256]{2,1,0:T(8,128)(2,1)S(1)}, u32[]{:S(2)}, u32[]{:S(2)}) %collective-permute-start.3) | collective-permute-done | bytes 442400 | tf_op jit(solution)/shard_map/ppermute | solution.py:606
  28.6 0.0 copy-done
  28.6 3.7 %shard_map.147 = (f32[6,256,128]{2,1,0:T(8,128)S(1)}, f32[256,256]{1,0:T(8,128)S(1)}, f32[8,128]{1,0:T(8,128)S(1)}) custom-call(bf16[3,288,256]{2,1,0:T(8,128)(2,1)S(1)} %pad_maximum_fusion.mid_ref, bf16[3,288,256]{2,1,0:T(8,128)(2,1)S(1)} %collective-permute-done.3.hi_ref, f32[8,384]{1,0:T(8,128)S(1)} %get-tuple-element.26.tab_ref, ...), custom_call_target="tpu_custom_call" | custom-call | flops 1000000000 | bytes 262144 | tf_op jit(solution)/shard_map/pallas_call | solution.py:635
  32.4 2.1 %collective-permute-done.2.lo_ref = bf16[3,288,256]{2,1,0:T(8,128)(2,1)S(1)} collective-permute-done((bf16[3,288,256]{2,1,0:T(8,128)(2,1)S(1)}, bf16[3,288,256]{2,1,0:T(8,128)(2,1)S(1)}, u32[]{:S(2)}, u32[]{:S(2)}) %collective-permute-start.2) | collective-permute-done | bytes 442400 | tf_op jit(solution)/shard_map/ppermute | solution.py:607
  34.5 3.5 %shard_map.148 = (f32[256,256]{1,0:T(8,128)S(1)}, f32[8,256]{1,0:T(8,128)S(1)}, f32[16,1,128]{2,1,0:T(1,128)S(1)}) custom-call(bf16[3,288,256]{2,1,0:T(8,128)(2,1)S(1)} %pad_maximum_fusion.mid_ref, bf16[3,288,256]{2,1,0:T(8,128)(2,1)S(1)} %collective-permute-done.2.lo_ref, bf16[1,1,256,256]{3,2,1,0:T(8,128)(2,1)S(1)} %copy-done, ...), custom_call_target="tpu_custom_call" | custom-call | flops 1000000000 | bytes 262144 | tf_op jit(solution)/shard_map/pallas_call | solution.py:642
  37.9 22.5 %all_to_all.10.got_ref = f32[16,1,128]{2,1,0:T(1,128)S(1)} all-to-all(f32[16,1,128]{2,1,0:T(1,128)S(1)} %get-tuple-element.35), channel_id=1, replica_groups=mesh['z'=8,'yh'=2,'c'=2,'yl'=4,'x'=4] {'z','c'}, dimensions={0} | all-to-all | bytes 16384 | tf_op jit(solution)/shard_map/all_to_all | solution.py:649
  60.5 12.9 %all_to_all.11.refs_0_ = f32[32,1,128]{2,1,0:T(1,128)S(1)} all-to-all(f32[32,1,128]{2,1,0:T(1,128)S(1)} %shard_map.149), channel_id=1, replica_groups=mesh['z'=8,'yh'=2,'c'=2,'yl'=4,'x'=4] {'yh','yl','x'}, dimensions={0} | all-to-all | bytes 32768 | tf_op jit(solution)/shard_map/all_to_all | solution.py:651
  73.4 0.8 %shard_map.150 = (f32[1,1,2,256]{3,2,1,0:T(2,128)}, f32[1,1,256]{2,1,0:T(1,128)}, f32[1,1,256,256]{3,2,1,0:T(8,128)}, f32[1,1,256]{2,1,0:T(1,128)}, f32[1,1,256]{2,1,0:T(1,128)}, /*index=5*/f32[1,1]{1,0:T(1,128)}) custom-call(f32[32,1,128]{2,1,0:T(1,128)S(1)} %all_to_all.11.refs_0_, f32[256,256]{1,0:T(8,128)S(1)} %get-tuple-element.36.refs_1_, ...), custom_call_target="tpu_custom_call" | custom-call | bytes 262144 | tf_op jit(solution)/shard_map/pallas_call | solution.py:652
  (1 shorter events, 0.0 us)
Async XLA Ops:
  0.6 28.0 %copy-start = (bf16[1,1,256,256]{3,2,1,0:T(8,128)(2,1)S(1)}, bf16[1,1,256,256]{3,2,1,0:T(8,128)(2,1)}, u32[]{:S(2)}) copy-start(bf16[1,1,256,256]{3,2,1,0:T(8,128)(2,1)} %w_ref.3) | copy-start | bytes 393220
  1.8 11.8 %collective-permute-start = (bf16[288,256]{1,0:T(8,128)(2,1)S(1)}, bf16[288,256]{1,0:T(8,128)(2,1)S(1)}, u32[]{:S(2)}, u32[]{:S(2)}) collective-permute-start(bf16[288,256]{1,0:T(8,128)(2,1)S(1)} %get-tuple-element.25), channel_id=1, source_target_pairs={{16,0},{32,16},{48,32},{64,48},{80,64},{96,80},{112,96},{128,112},... | collective-permute-start | bytes 442376 | tf_op jit(solution)/shard_map/ppermute | solution.py:601
  10.6 5.1 %collective-permute-start.1 = (bf16[288,256]{1,0:T(8,128)(2,1)S(1)}, bf16[288,256]{1,0:T(8,128)(2,1)S(1)}, u32[]{:S(2)}, u32[]{:S(2)}) collective-permute-start(bf16[288,256]{1,0:T(8,128)(2,1)S(1)} %get-tuple-element.25), channel_id=1, source_target_pairs={{0,16},{16,32},{32,48},{48,64},{64,80},{80,96},{96,112},{112,128},... | collective-permute-start | bytes 442376 | tf_op jit(solution)/shard_map/ppermute | solution.py:602
  15.7 12.9 %collective-permute-start.3 = (bf16[3,288,256]{2,1,0:T(8,128)(2,1)S(1)}, bf16[3,288,256]{2,1,0:T(8,128)(2,1)S(1)}, u32[]{:S(2)}, u32[]{:S(2)}) collective-permute-start(bf16[3,288,256]{2,1,0:T(8,128)(2,1)S(1)} %pad_maximum_fusion.mid_ref), channel_id=1, source_target_pairs={{0,1},{1,0},{2,3},{3,2},{4,5},{5,4},{6,7},{7,6},{8,9},{9,8},{10,11... | collective-permute-start | bytes 1327112 | tf_op jit(solution)/shard_map/ppermute | solution.py:606
  18.9 15.6 %collective-permute-start.2 = (bf16[3,288,256]{2,1,0:T(8,128)(2,1)S(1)}, bf16[3,288,256]{2,1,0:T(8,128)(2,1)S(1)}, u32[]{:S(2)}, u32[]{:S(2)}) collective-permute-start(bf16[3,288,256]{2,1,0:T(8,128)(2,1)S(1)} %pad_maximum_fusion.mid_ref), channel_id=1, source_target_pairs={{1,2},{3,4},{5,6},{7,8},{9,10},{11,12},{13,14},{15,0},{2,1},{4,3},... | collective-permute-start | bytes 1327112 | tf_op jit(solution)/shard_map/ppermute | solution.py:607
